TPU v7x, 128 devices: a whole 4x4x4 slice. The times are simulated.
128 devices in a mesh: group: 4 (over y), member: 32 (over z, x, core).
Axes of the slice: x: 4, y: 4, z: 4, core: 2. Of those that a mesh axis runs over, the one named last changes fastest.
Arguments:
- tokens: bfloat16 [256, 256, 1280], P(('group', 'member')), may hold values from -12 to 12
- slot_key_matrix: bfloat16 [1280, 128], replicated, may hold values from -2.5 to 2.5
- w_in: bfloat16 [128, 1280, 2560], P(('group', 'member')), may hold values from -0.15625 to 0.15625
- w_out: bfloat16 [128, 2560, 1280], P(('group', 'member')), may hold values from -0.125 to 0.125
- upstream: bfloat16 [256, 256, 1280], P(('group', 'member')), may hold values from -6 to 6
Outputs:
- mixed: bfloat16 [256, 256, 1280], P(('group', 'member'))
- token_grad: bfloat16 [256, 256, 1280], P(('group', 'member'))
- key_grad: float32 [128, 1280], P(('group', 'member'))
All inputs are finite; a program needn't handle non-finite values.
Results may differ from a plain program's by a relative error of at most 0.014.
Values may be sent and summed in bfloat16 or wider, within the bound.
No kernel may reach another device: no remote copies, remote signals or barrier semaphores. Data moves between devices by JAX's collectives and lax.ppermute only.
A program may use at most 64 MiB of HBM per device.

v0:
```python
import jax
import jax.numpy as jnp
from jax import lax
from jax.sharding import PartitionSpec as P


def gelu_tanh(value):
    return jax.nn.gelu(value, approximate=True)


def to_experts(slot_inputs):
    slots_per_device, slot_count, feature_width = slot_inputs.shape
    arrived = lax.all_to_all(
        slot_inputs, ("group", "member"), split_axis=1, concat_axis=0, tiled=True
    )
    return arrived.reshape(-1, feature_width)


def to_images(slot_row_block):
    feature_width = slot_row_block.shape[1]
    return lax.all_to_all(
        slot_row_block.reshape(-1, 1, feature_width),
        ("group", "member"),
        split_axis=0,
        concat_axis=1,
        tiled=True,
    )


def shards(tokens, slot_key_matrix, w_in, w_out, upstream):
    logits = jnp.einsum("imd,ds->ims", tokens, slot_key_matrix, preferred_element_type=jnp.float32)
    dispatch = jax.nn.softmax(logits, axis=1)
    combine = jax.nn.softmax(logits, axis=2)
    dispatch_b = dispatch.astype(jnp.bfloat16)
    combine_b = combine.astype(jnp.bfloat16)
    slot_in = jnp.einsum(
        "ims,imd->isd", dispatch_b, tokens, preferred_element_type=jnp.float32
    ).astype(jnp.bfloat16)
    d_slot_out = jnp.einsum(
        "ims,imd->isd", combine_b, upstream, preferred_element_type=jnp.float32
    ).astype(jnp.bfloat16)
    first_w = w_in[0]
    second_w = w_out[0]
    slot_row_block = to_experts(slot_in)
    pre_act = jnp.dot(slot_row_block, first_w, preferred_element_type=jnp.float32)
    activated = gelu_tanh(pre_act).astype(jnp.bfloat16)
    out_rows = jnp.dot(activated, second_w, preferred_element_type=jnp.float32).astype(jnp.bfloat16)
    returned = to_images(out_rows)
    mixed = jnp.einsum(
        "ims,isd->imd", combine_b, returned, preferred_element_type=jnp.float32
    ).astype(jnp.bfloat16)
    d_combine = jnp.einsum("imd,isd->ims", upstream, returned, preferred_element_type=jnp.float32)
    d_logit_c = combine * (d_combine - jnp.sum(combine * d_combine, axis=2, keepdims=True))
    grad_rows = to_experts(d_slot_out)
    d_act = jnp.einsum("rd,fd->rf", grad_rows, second_w, preferred_element_type=jnp.float32)
    d_pre = jax.vjp(gelu_tanh, pre_act)[1](d_act)[0].astype(jnp.bfloat16)
    back_rows = jnp.einsum("rf,df->rd", d_pre, first_w, preferred_element_type=jnp.float32).astype(
        jnp.bfloat16
    )
    d_slot_in = to_images(back_rows)
    d_dispatch = jnp.einsum("imd,isd->ims", tokens, d_slot_in, preferred_element_type=jnp.float32)
    d_logit_d = dispatch * (d_dispatch - jnp.sum(dispatch * d_dispatch, axis=1, keepdims=True))
    d_logits = (d_logit_c + d_logit_d).astype(jnp.bfloat16)
    token_grad = jnp.einsum(
        "ims,ds->imd", d_logits, slot_key_matrix, preferred_element_type=jnp.float32
    )
    token_grad = token_grad + jnp.einsum(
        "ims,isd->imd", dispatch_b, d_slot_in, preferred_element_type=jnp.float32
    )
    token_grad = token_grad.astype(jnp.bfloat16)
    key_grad = lax.psum_scatter(
        jnp.einsum("ims,imd->sd", d_logits, tokens, preferred_element_type=jnp.float32),
        ("group", "member"),
        scatter_dimension=0,
        tiled=True,
    )
    return (mixed, token_grad, key_grad)


def solution(mesh):
    in_specs = (
        P(("group", "member"), None, None),
        P(),
        P(("group", "member"), None, None),
        P(("group", "member"), None, None),
        P(("group", "member"), None, None),
    )
    out_specs = (
        P(("group", "member"), None, None),
        P(("group", "member"), None, None),
        P(("group", "member"), None),
    )
    return jax.shard_map(shards, mesh=mesh, in_specs=in_specs, out_specs=out_specs, check_vma=False)
```

profile of v0, /device:TPU:1, one launch (start us, length us, event | category | flops | bytes accessed | tf_op | source)
XLA Modules:
  0.0 294.8 jit_solution(341062676818129515)
XLA Ops:
  11.2 1.5 copy.34
  12.7 11.5 %all-to-all-start = ((bf16[2,128,1280]{2,0,1:T(2,128)(2,1)}), bf16[2,128,1280]{2,0,1:T(2,128)(2,1)S(1)}, u32[]{:S(2)}, u32[]{:S(2)}) async-start(bf16[2,128,1280]{2,0,1:T(2,128)(2,1)} %copy.34), calls=%async_computation | async-start | bytes 1310720 | tf_op jit(solution)/shard_map/all_to_all | solution.py:13
  25.1 2.5 convolution_convert_fusion.1
  27.6 1.5 copy.39
  29.1 10.2 %all-to-all-done = bf16[2,128,1280]{2,0,1:T(2,128)(2,1)S(1)} async-done(((bf16[2,128,1280]{2,0,1:T(2,128)(2,1)}), bf16[2,128,1280]{2,0,1:T(2,128)(2,1)S(1)}, u32[]{:S(2)}, u32[]{:S(2)}) %all-to-all-start) | async-done | bytes 655392 | tf_op jit(solution)/shard_map/all_to_all | solution.py:13
  39.3 4.5 %all-to-all-start.2 = ((bf16[2,128,1280]{2,0,1:T(2,128)(2,1)}), bf16[2,128,1280]{2,0,1:T(2,128)(2,1)S(1)}, u32[]{:S(2)}, u32[]{:S(2)}) async-start(bf16[2,128,1280]{2,0,1:T(2,128)(2,1)} %copy.39), calls=%async_computation.2 | async-start | bytes 1310720 | tf_op jit(solution)/shard_map/all_to_all | solution.py:13
  44.1 14.9 %all-to-all-done.2 = bf16[2,128,1280]{2,0,1:T(2,128)(2,1)S(1)} async-done(((bf16[2,128,1280]{2,0,1:T(2,128)(2,1)}), bf16[2,128,1280]{2,0,1:T(2,128)(2,1)S(1)}, u32[]{:S(2)}, u32[]{:S(2)}) %all-to-all-start.2) | async-done | bytes 655392 | tf_op jit(solution)/shard_map/all_to_all | solution.py:13
  59.2 6.2 %fusion.10 = f32[256,2560]{1,0:T(8,128)} fusion(bf16[256,1280]{1,0:T(8,128)(2,1)S(1)} %reshape.26, bf16[1,1280,2560]{2,1,0:T(8,128)(2,1)} %param.7), kind=kOutput, calls=%fused_computation.10 | convolution fusion | flops 1677721600 | bytes 9830400 | tf_op jit(solution)/shard_map/dot_general | solution.py:45
  65.4 9.8 %fusion.31 = bf16[256,1,1280]{2,0,1:T(8,128)(2,1)S(1)} fusion(bf16[1,1280,2560]{2,1,0:T(8,128)(2,1)} %param.7, f32[256,2560]{1,0:T(8,128)} %fusion.10, bf16[256,1280]{1,0:T(8,128)(2,1)S(1)} %reshape.28, bf16[1,2560,1280]{2,1,0:T(8,128)(2,1)} %param.8), kind=kOutput, calls=%fused_computation.30 | convolution fusion | flops 3368878080 | bytes 17039360 | tf_op jit(solution)/shard_map/rf,df->rd/dot_general | solution.py:57
  78.0 4.5 %all-to-all-start.3 = ((bf16[128,2,1280]{2,1,0:T(2,128)(2,1)}), bf16[128,2,1280]{2,1,0:T(2,128)(2,1)S(1)}, u32[]{:S(2)}, u32[]{:S(2)}) async-start(bf16[128,2,1280]{2,1,0:T(2,128)(2,1)} %reshape.36), calls=%async_computation.3 | async-start | bytes 1310720 | tf_op jit(solution)/shard_map/all_to_all | solution.py:21
  82.4 6.0 %fusion.28 = bf16[256,1,1280]{2,0,1:T(8,128)(2,1)S(1)} fusion(bf16[1,2560,1280]{2,1,0:T(8,128)(2,1)} %param.8, f32[256,2560]{1,0:T(8,128)} %fusion.10), kind=kOutput, calls=%fused_computation.29 | convolution fusion | flops 1683947520 | bytes 9830400 | tf_op jit(solution)/shard_map/dot_general | solution.py:47
  90.6 6.9 %all-to-all-done.3 = bf16[128,2,1280]{2,1,0:T(2,128)(2,1)S(1)} async-done(((bf16[128,2,1280]{2,1,0:T(2,128)(2,1)}), bf16[128,2,1280]{2,1,0:T(2,128)(2,1)S(1)}, u32[]{:S(2)}, u32[]{:S(2)}) %all-to-all-start.3) | async-done | bytes 655392 | tf_op jit(solution)/shard_map/all_to_all | solution.py:21
  97.6 5.3 %all-to-all-start.1 = ((bf16[128,2,1280]{2,1,0:T(2,128)(2,1)}), bf16[128,2,1280]{2,1,0:T(2,128)(2,1)}, u32[]{:S(2)}, u32[]{:S(2)}) async-start(bf16[128,2,1280]{2,1,0:T(2,128)(2,1)} %reshape.34), calls=%async_computation.1 | async-start | bytes 1310720 | tf_op jit(solution)/shard_map/all_to_all | solution.py:21
  103.5 4.0 %reduce.1 = bf16[256,1280]{1,0:T(8,128)(2,1)S(1)} reduce(bf16[256,1,1280]{2,1,0:T(2,128)(2,1)S(1)} %reshape.37, bf16[]{:T(256)} %constant.25), dimensions={1}, to_apply=%all_to_all.58.reduce_sub_computation | reduce | bytes 1310722 | tf_op jit(solution)/shard_map/all_to_all | solution.py:21
  108.9 8.9 %all-to-all-done.1 = bf16[128,2,1280]{2,1,0:T(2,128)(2,1)} async-done(((bf16[128,2,1280]{2,1,0:T(2,128)(2,1)}), bf16[128,2,1280]{2,1,0:T(2,128)(2,1)}, u32[]{:S(2)}, u32[]{:S(2)}) %all-to-all-start.1) | async-done | bytes 655392 | tf_op jit(solution)/shard_map/all_to_all | solution.py:21
  117.8 4.1 %reshape.35 = bf16[256,1,1280]{2,1,0:T(2,128)(2,1)S(1)} reshape(bf16[128,2,1280]{2,1,0:T(2,128)(2,1)} %all-to-all-done.1) | data formatting | bytes 1310720
  121.9 4.8 %reduce = bf16[256,1280]{1,0:T(8,128)(2,1)} reduce(bf16[256,1,1280]{2,1,0:T(2,128)(2,1)S(1)} %reshape.35, bf16[]{:T(256)} %constant.25), dimensions={1}, to_apply=%all_to_all.51.reduce_sub_computation | reduce | bytes 1310722 | tf_op jit(solution)/shard_map/all_to_all | solution.py:21
  126.7 2.2 all_to_all.52
  128.9 2.5 convolution_bitcast_fusion.2
  132.8 4.6 %convolution_bitcast_fusion = f32[128,1280]{1,0:T(8,128)} fusion(bf16[2,256,1280]{2,1,0:T(8,128)(2,1)S(1)} %copy-done, f32[2,256,128]{2,1,0:T(8,128)S(1)} %fusion.44, f32[2,256,128]{2,1,0:T(8,128)} %convolution_bitcast_fusion.2, f32[2,256,128]{2,1,0:T(8,128)} %get-tuple-element.6, f32[2,256]{1,0:T(2,128)S(1)} %get-tuple-element.5), kind=kOutput, calls=%fused_computation.31 | convolution fusion | flops 168231552 | bytes 2754560 | tf_op jit(solution)/shard_map/ims,imd->sd/dot_general | solution.py:72
  137.4 4.9 %fusion.50 = f32[2,256,1280]{2,1,0:T(8,128)} fusion(f32[2,256,128]{2,1,0:T(8,128)S(1)} %fusion.44, f32[2,256,128]{2,1,0:T(8,128)} %convolution_bitcast_fusion.2, bf16[1280,128]{1,0:T(8,128)(2,1)S(1)} %copy-done.1, f32[2,256,128]{2,1,0:T(8,128)} %get-tuple-element.6, f32[2,256]{1,0:T(2,128)S(1)} %get-tuple-element.5), kind=kOutput, calls=%fused_computation.48 | convolution fusion | flops 168231552 | bytes 3737600 | tf_op jit(solution)/shard_map/ims,ds->imd/dot_general | solution.py:64
  142.3 2.3 convolution_convert_fusion
  144.6 3.3 %fusion.12 = bf16[2,256,1280]{2,1,0:T(8,128)(2,1)} fusion(f32[2,256,1280]{2,1,0:T(8,128)} %fusion.50, bf16[128,2,1,1280]{3,1,0,2:T(2,128)(2,1)S(1)} %all_to_all.59, f32[2,128]{1,0:T(2,128)S(1)} %get-tuple-element.3, f32[2,256,128]{2,1,0:T(8,128)S(1)} %fusion.64), kind=kOutput, calls=%fused_computation.15 | convolution fusion | flops 169280000 | bytes 4850688 | tf_op jit(solution)/shard_map/ims,isd->imd/dot_general | solution.py:67
  147.9 138.6 %all-reduce.3.cloned.1.call-done = f32[128,1280]{1,0:T(8,128)} async-done(((f32[128,1280]{1,0:T(8,128)}), f32[128,1280]{1,0:T(8,128)}) %all-reduce.3.cloned.1.call-update) | async-done | bytes 655376
  (22 shorter events, 15.0 us)
Async XLA Ops:
  7.2 1.3 copy-start
  12.7 26.6 %all-to-all-start = ((bf16[2,128,1280]{2,0,1:T(2,128)(2,1)}), bf16[2,128,1280]{2,0,1:T(2,128)(2,1)S(1)}, u32[]{:S(2)}, u32[]{:S(2)}) async-start(bf16[2,128,1280]{2,0,1:T(2,128)(2,1)} %copy.34), calls=%async_computation | async-start | bytes 1310720 | tf_op jit(solution)/shard_map/all_to_all | solution.py:13
  39.3 19.6 %all-to-all-start.2 = ((bf16[2,128,1280]{2,0,1:T(2,128)(2,1)}), bf16[2,128,1280]{2,0,1:T(2,128)(2,1)S(1)}, u32[]{:S(2)}, u32[]{:S(2)}) async-start(bf16[2,128,1280]{2,0,1:T(2,128)(2,1)} %copy.39), calls=%async_computation.2 | async-start | bytes 1310720 | tf_op jit(solution)/shard_map/all_to_all | solution.py:13
  78.0 19.6 %all-to-all-start.3 = ((bf16[128,2,1280]{2,1,0:T(2,128)(2,1)}), bf16[128,2,1280]{2,1,0:T(2,128)(2,1)S(1)}, u32[]{:S(2)}, u32[]{:S(2)}) async-start(bf16[128,2,1280]{2,1,0:T(2,128)(2,1)} %reshape.36), calls=%async_computation.3 | async-start | bytes 1310720 | tf_op jit(solution)/shard_map/all_to_all | solution.py:21
  97.6 20.3 %all-to-all-start.1 = ((bf16[128,2,1280]{2,1,0:T(2,128)(2,1)}), bf16[128,2,1280]{2,1,0:T(2,128)(2,1)}, u32[]{:S(2)}, u32[]{:S(2)}) async-start(bf16[128,2,1280]{2,1,0:T(2,128)(2,1)} %reshape.34), calls=%async_computation.1 | async-start | bytes 1310720 | tf_op jit(solution)/shard_map/all_to_all | solution.py:21
  102.9 183.7 %all-reduce.3.cloned.1.call-start = ((), (), s32[]{:S(2)}) async-start(), calls=%async_computation.4 | async-start | bytes 1310720
  131.4 6.0 %copy-start.1 = (bf16[1280,128]{1,0:T(8,128)(2,1)S(1)}, bf16[1280,128]{1,0:T(8,128)(2,1)}, u32[]{:S(2)}) copy-start(bf16[1280,128]{1,0:T(8,128)(2,1)} %param.6) | copy-start | bytes 983044
Sparse Core Ops, SparseCore 0:
  144.7 141.8 all-reduce.2
where the time goes:
time: 296 us; the launch traced here: 295 us
  waiting for transfers between devices  180 us (61%)
  matrix products  45.3 us (15%)
  starting transfers between devices  25.8 us (9%)
  local copies, waits for them, and re-layouts  15.9 us (5%)
  between operations  14.2 us (5%)
  other arithmetic  14 us (5%)
    unnamed x2, waiting for transfers between devices  139 us
    all_to_all x2, waiting for transfers between devices, to_experts(): lax.all_to_all(slot_inputs, ('group', 'member'), split_axis=1, concat_axi...  25.1 us
    all_to_all x2, starting transfers between devices, to_experts(): lax.all_to_all(slot_inputs, ('group', 'member'), split_axis=1, concat_axi...  16 us
    all_to_all x2, waiting for transfers between devices, to_images(): lax.all_to_all(slot_row_block.reshape(-1, 1, feature_width), ('group', 'm...  15.8 us
    dot_general x1, matrix products, shards(): jnp.einsum('rf,df->rd', d_pre, first_w, preferred_element_type=jnp.float32)  9.82 us
    all_to_all x2, starting transfers between devices, to_images(): lax.all_to_all(slot_row_block.reshape(-1, 1, feature_width), ('group', 'm...  9.75 us
    unnamed x9, local copies, waits for them, and re-layouts  9.47 us
    all_to_all x2, other arithmetic, to_images(): lax.all_to_all(slot_row_block.reshape(-1, 1, feature_width), ('group', 'm...  8.77 us
  transfers between devices with their start and end apart: 5, of which 5 were waited for; matrix products, arithmetic and copies ran while one was open for 8% of the time, Pallas kernels for 0%

commit v1 on v0

v1 whole, which is shorter than its diff:
```python
import jax
import jax.numpy as jnp
from jax import lax
from jax.experimental import pallas as pl
from jax.experimental.pallas import tpu as pltpu
from jax.sharding import PartitionSpec as P

AXES = ("group", "member")
HALVES = 2
LANES = 128
KINDS = 2
CHUNK = 512
VMEM_LIMIT = 48 * 1024 * 1024
GELU_SCALE = 0.7978845608028654
GELU_CUBIC = 0.044715


def row_dot(a, b):
    return lax.dot_general(a, b, (((1,), (0,)), ((), ())), preferred_element_type=jnp.float32)


def row_dot_t(a, b):
    return lax.dot_general(a, b, (((1,), (1,)), ((), ())), preferred_element_type=jnp.float32)


def col_dot(a, b):
    return lax.dot_general(a, b, (((0,), (0,)), ((), ())), preferred_element_type=jnp.float32)


def place(spread, kind, image, images, rows):
    peers, width = rows.shape
    per_peer = KINDS * images * HALVES
    lane_blocks = spread.shape[0]
    for half in range(HALVES):
        at = (kind * images + image) * HALVES + half
        for block in range(lane_blocks):
            first = (half * lane_blocks + block) * LANES
            spread[block, pl.ds(at, peers, stride=per_peer), :] = rows[:, first : first + LANES]


def pick(spread, kind, image, images, peers):
    per_peer = KINDS * images * HALVES
    parts = []
    for half in range(HALVES):
        at = (kind * images + image) * HALVES + half
        for block in range(spread.shape[0]):
            rows = spread[block, pl.ds(at, peers, stride=per_peer), :]
            parts.append(rows.astype(jnp.bfloat16))
    return jnp.concatenate(parts, axis=1)


def widen(spread, arrived):
    for block in range(spread.shape[0]):
        lanes = slice(block * LANES, (block + 1) * LANES)
        spread[block] = arrived[:, lanes].astype(jnp.float32)


def narrow(sent, spread):
    for block in range(spread.shape[0]):
        lanes = slice(block * LANES, (block + 1) * LANES)
        sent[:, lanes] = spread[block].astype(jnp.bfloat16)


def spread_shape(rows, part):
    return pltpu.VMEM((part // LANES, rows, LANES), jnp.float32)


def route_kernel(
    tokens_hbm, upstream_hbm, key_hbm, sent, dispatch, combine, tokens, upstream, key, spread, sems
):
    images = tokens.shape[0]
    key_copy = pltpu.make_async_copy(key_hbm, key, sems.at[2 * images])
    key_copy.start()
    copies = []
    for image in range(images):
        for place_at, (source, target) in enumerate(((tokens_hbm, tokens), (upstream_hbm, upstream))):
            copy = pltpu.make_async_copy(
                source.at[image], target.at[image], sems.at[2 * image + place_at]
            )
            copy.start()
            copies.append(copy)
    key_copy.wait()
    for image in range(images):
        copies[2 * image].wait()
        logits = row_dot(tokens[image], key[...])
        by_token = jnp.exp(logits - jnp.max(logits, axis=0, keepdims=True))
        by_token = by_token / jnp.sum(by_token, axis=0, keepdims=True)
        dispatch[image] = by_token
        slot_in = col_dot(by_token.astype(jnp.bfloat16), tokens[image])
        place(spread, 0, image, images, slot_in)
        by_slot = jnp.exp(logits - jnp.max(logits, axis=1, keepdims=True))
        by_slot = by_slot / jnp.sum(by_slot, axis=1, keepdims=True)
        combine[image] = by_slot
        copies[2 * image + 1].wait()
        d_slot_out = col_dot(by_slot.astype(jnp.bfloat16), upstream[image])
        place(spread, 1, image, images, d_slot_out)
    narrow(sent, spread)


def route(tokens, upstream, slot_key_matrix):
    images, patches, width = tokens.shape
    slots = slot_key_matrix.shape[1]
    rows = slots * KINDS * images * HALVES
    part = width // HALVES
    return pl.pallas_call(
        route_kernel,
        out_shape=(
            jax.ShapeDtypeStruct((rows, part), jnp.bfloat16),
            jax.ShapeDtypeStruct((images, patches, slots), jnp.float32),
            jax.ShapeDtypeStruct((images, patches, slots), jnp.float32),
        ),
        in_specs=[pl.BlockSpec(memory_space=pl.ANY)] * 3,
        out_specs=(pl.BlockSpec(memory_space=pltpu.VMEM),) * 3,
        scratch_shapes=[
            pltpu.VMEM(tokens.shape, tokens.dtype),
            pltpu.VMEM(upstream.shape, upstream.dtype),
            pltpu.VMEM(slot_key_matrix.shape, slot_key_matrix.dtype),
            spread_shape(rows, part),
            pltpu.SemaphoreType.DMA((2 * images + 1,)),
        ],
        compiler_params=pltpu.CompilerParams(vmem_limit_bytes=VMEM_LIMIT),
        name="route",
    )(tokens, upstream, slot_key_matrix)


def expert_kernel(
    images, arrived, w_in_hbm, w_out_hbm, sent, w_in, w_out, spread, rows_in, rows_grad, out, back, sems
):
    steps, width, chunk = w_in.shape
    peers = arrived.shape[0] // (KINDS * images * HALVES)

    def weight_copies(step):
        at = pl.multiple_of(step * chunk, chunk)
        return (
            pltpu.make_async_copy(
                w_in_hbm.at[0, :, pl.ds(at, chunk)], w_in.at[step], sems.at[0, step]
            ),
            pltpu.make_async_copy(
                w_out_hbm.at[0, pl.ds(at, chunk), :], w_out.at[step], sems.at[1, step]
            ),
        )

    def begin(step, carry):
        for copy in weight_copies(step):
            copy.start()
        return carry

    lax.fori_loop(0, steps, begin, 0)
    widen(spread, arrived)
    for image in range(images):
        rows = pl.ds(image * peers, peers)
        rows_in[rows, :] = pick(spread, 0, image, images, peers)
        rows_grad[rows, :] = pick(spread, 1, image, images, peers)
    out[...] = jnp.zeros_like(out)
    back[...] = jnp.zeros_like(back)

    def one(step, carry):
        for copy in weight_copies(step):
            copy.wait()
        pre = row_dot(rows_in[...], w_in[step])
        square = pre * pre
        tanh = jnp.tanh(GELU_SCALE * (pre * (1.0 + GELU_CUBIC * square)))
        gate = 0.5 * (1.0 + tanh)
        activated = (pre * gate).astype(jnp.bfloat16)
        slope = gate + 0.5 * pre * (1.0 - tanh * tanh) * (
            GELU_SCALE * (1.0 + 3.0 * GELU_CUBIC * square)
        )
        out[...] += row_dot(activated, w_out[step])
        d_act = row_dot_t(rows_grad[...], w_out[step])
        d_pre = (d_act * slope).astype(jnp.bfloat16)
        back[...] += row_dot_t(d_pre, w_in[step])
        return carry

    lax.fori_loop(0, steps, one, 0)
    for image in range(images):
        rows = pl.ds(image * peers, peers)
        place(spread, 0, image, images, out[rows, :])
        place(spread, 1, image, images, back[rows, :])
    narrow(sent, spread)


def expert(arrived, w_in, w_out, images):
    _, width, hidden = w_in.shape
    steps = hidden // CHUNK
    rows = arrived.shape[0] // (KINDS * HALVES)

    def body(*refs):
        expert_kernel(images, *refs)

    return pl.pallas_call(
        body,
        out_shape=jax.ShapeDtypeStruct(arrived.shape, jnp.bfloat16),
        in_specs=[
            pl.BlockSpec(memory_space=pltpu.VMEM),
            pl.BlockSpec(memory_space=pl.ANY),
            pl.BlockSpec(memory_space=pl.ANY),
        ],
        out_specs=pl.BlockSpec(memory_space=pltpu.VMEM),
        scratch_shapes=[
            pltpu.VMEM((steps, width, CHUNK), w_in.dtype),
            pltpu.VMEM((steps, CHUNK, width), w_out.dtype),
            spread_shape(*arrived.shape),
            pltpu.VMEM((rows, width), jnp.bfloat16),
            pltpu.VMEM((rows, width), jnp.bfloat16),
            pltpu.VMEM((rows, width), jnp.float32),
            pltpu.VMEM((rows, width), jnp.float32),
            pltpu.SemaphoreType.DMA((2, steps)),
        ],
        compiler_params=pltpu.CompilerParams(vmem_limit_bytes=VMEM_LIMIT),
        name="expert",
    )(arrived, w_in, w_out)


def logit_grad_kernel(
    arrived, tokens, upstream, dispatch, combine, d_logits, key_part, spread, spread_key
):
    images, patches, width = tokens.shape
    slots = dispatch.shape[2]
    widen(spread, arrived)
    total = jnp.zeros((slots, width), jnp.float32)
    for image in range(images):
        returned = pick(spread, 0, image, images, slots)
        d_slot_in = pick(spread, 1, image, images, slots)
        d_combine = row_dot_t(upstream[image], returned)
        by_slot = combine[image]
        both = by_slot * (d_combine - jnp.sum(by_slot * d_combine, axis=1, keepdims=True))
        d_dispatch = row_dot_t(tokens[image], d_slot_in)
        by_token = dispatch[image]
        both += by_token * (d_dispatch - jnp.sum(by_token * d_dispatch, axis=0, keepdims=True))
        both = both.astype(jnp.bfloat16)
        d_logits[image] = both
        total += col_dot(both, tokens[image])
    lane_blocks = spread_key.shape[0]
    for half in range(HALVES):
        for block in range(lane_blocks):
            first = (half * lane_blocks + block) * LANES
            lanes = total[:, first : first + LANES]
            spread_key[block, pl.ds(half, slots, stride=HALVES), :] = lanes
    narrow(key_part, spread_key)


def logit_grad(arrived, tokens, upstream, dispatch, combine):
    images, patches, width = tokens.shape
    slots = dispatch.shape[2]
    key_shape = (slots * HALVES, width // HALVES)
    return pl.pallas_call(
        logit_grad_kernel,
        out_shape=(
            jax.ShapeDtypeStruct(dispatch.shape, jnp.bfloat16),
            jax.ShapeDtypeStruct(key_shape, jnp.bfloat16),
        ),
        in_specs=[pl.BlockSpec(memory_space=pltpu.VMEM)] * 5,
        out_specs=(pl.BlockSpec(memory_space=pltpu.VMEM),) * 2,
        scratch_shapes=[
            spread_shape(*arrived.shape),
            spread_shape(*key_shape),
        ],
        compiler_params=pltpu.CompilerParams(vmem_limit_bytes=VMEM_LIMIT),
        name="logit_grad",
    )(arrived, tokens, upstream, dispatch, combine)


def finish_kernel(arrived, dispatch, combine, d_logits, key, mixed, token_grad, spread):
    images, patches, slots = dispatch.shape
    widen(spread, arrived)
    for image in range(images):
        returned = pick(spread, 0, image, images, slots)
        mixed[image] = row_dot(combine[image].astype(jnp.bfloat16), returned).astype(jnp.bfloat16)
        d_slot_in = pick(spread, 1, image, images, slots)
        grad = row_dot_t(d_logits[image], key[...])
        grad += row_dot(dispatch[image].astype(jnp.bfloat16), d_slot_in)
        token_grad[image] = grad.astype(jnp.bfloat16)


def finish(arrived, dispatch, combine, d_logits, slot_key_matrix):
    images, patches, slots = dispatch.shape
    width = slot_key_matrix.shape[0]
    shape = jax.ShapeDtypeStruct((images, patches, width), jnp.bfloat16)
    return pl.pallas_call(
        finish_kernel,
        out_shape=(shape, shape),
        in_specs=[pl.BlockSpec(memory_space=pltpu.VMEM)] * 5,
        out_specs=(pl.BlockSpec(memory_space=pltpu.VMEM),) * 2,
        scratch_shapes=[spread_shape(*arrived.shape)],
        compiler_params=pltpu.CompilerParams(vmem_limit_bytes=VMEM_LIMIT),
        name="finish",
    )(arrived, dispatch, combine, d_logits, slot_key_matrix)


def exchange(rows, peers):
    blocks = rows.reshape(peers, -1, rows.shape[1])
    blocks = lax.all_to_all(blocks, AXES, split_axis=0, concat_axis=0, tiled=True)
    return blocks.reshape(rows.shape)


def shards(tokens, slot_key_matrix, w_in, w_out, upstream):
    images, patches, width = tokens.shape
    slots = slot_key_matrix.shape[1]
    sent, dispatch, combine = route(tokens, upstream, slot_key_matrix)
    arrived = exchange(sent, slots)
    answered = expert(arrived, w_in, w_out, images)
    returned = exchange(answered, slots)
    d_logits, key_part = logit_grad(returned, tokens, upstream, dispatch, combine)
    key_terms = exchange(key_part, slots)
    mixed, token_grad = finish(returned, dispatch, combine, d_logits, slot_key_matrix)
    key_grad = jnp.sum(key_terms.reshape(slots, 1, width).astype(jnp.float32), axis=0)
    return (mixed, token_grad, key_grad)


def solution(mesh):
    in_specs = (
        P(AXES, None, None),
        P(),
        P(AXES, None, None),
        P(AXES, None, None),
        P(AXES, None, None),
    )
    out_specs = (P(AXES, None, None), P(AXES, None, None), P(AXES, None))
    return jax.shard_map(shards, mesh=mesh, in_specs=in_specs, out_specs=out_specs, check_vma=False)
```

time: 296 us -> 98.4 us (0.33)
  waiting for transfers between devices: 180 us -> 9.18 us
  blocking collectives: 0 us -> 59.7 us
  matrix products: 45.3 us -> 0 us
  starting transfers between devices: 25.8 us -> 4.28 us
  Pallas kernels: 0 us -> 18.9 us
  other arithmetic: 14 us -> 0.32 us
  between operations: 14.2 us -> 0.71 us
  local copies, waits for them, and re-layouts: 15.9 us -> 5.06 us
    unnamed x2 -> x0, waiting for transfers between devices: 139 us -> none
    all_to_all x0 -> x2, blocking collectives: none -> 59.7 us  [exchange(): lax.all_to_all(blocks, AXES, split_axis=0, concat_axis=0, tiled=True)]
    dot_general x12 -> x0, matrix products: 45.3 us -> none  [the longest x1 9.82 us: shards(): jnp.einsum('rf,df->rd', d_pre, first_w, preferred_element_type=jnp.float32)]
    all_to_all x4 -> x1, waiting for transfers between devices: 41 us -> 9.18 us  [exchange(): lax.all_to_all(blocks, AXES, split_axis=0, concat_axis=0, tiled=True)]
    all_to_all x4 -> x1, starting transfers between devices: 25.7 us -> 4.28 us  [exchange(): lax.all_to_all(blocks, AXES, split_axis=0, concat_axis=0, tiled=True)]
    pallas_call x0 -> x4, Pallas kernels: none -> 18.9 us  [the longest x1 11.5 us: expert(): pl.pallas_call(body, out_shape=jax.ShapeDtypeStruct(arrived.shape, jnp.bf...]
    all_to_all x2 -> x0, other arithmetic: 8.77 us -> none  [to_images(): lax.all_to_all(slot_row_block.reshape(-1, 1, feature_width), ('group', 'm...]
    unnamed x9 -> x13, local copies, waits for them, and re-layouts: 9.47 us -> 4.22 us
  transfers between devices with their start and end apart: 5 -> 1, of which waited for: 5 -> 1; matrix products, arithmetic and copies ran while one was open for 8% -> 0% of each run, Pallas kernels for 0% -> 3%
where the time goes in v1:
time: 98.4 us; the launch traced here: 98.1 us
  blocking collectives  59.7 us (61%)
  Pallas kernels  18.9 us (19%)
  waiting for transfers between devices  9.18 us (9%)
  local copies, waits for them, and re-layouts  5.06 us (5%)
  starting transfers between devices  4.28 us (4%)
    all_to_all x2, blocking collectives, exchange(): lax.all_to_all(blocks, AXES, split_axis=0, concat_axis=0, tiled=True)  59.7 us
    pallas_call x1, Pallas kernels, expert(): pl.pallas_call(body, out_shape=jax.ShapeDtypeStruct(arrived.shape, jnp.bf...  11.5 us
    all_to_all x1, waiting for transfers between devices, exchange(): lax.all_to_all(blocks, AXES, split_axis=0, concat_axis=0, tiled=True)  9.18 us
    all_to_all x1, starting transfers between devices, exchange(): lax.all_to_all(blocks, AXES, split_axis=0, concat_axis=0, tiled=True)  4.28 us
    unnamed x13, local copies, waits for them, and re-layouts  4.22 us
    pallas_call x1, Pallas kernels, route(): pl.pallas_call(route_kernel, out_shape=(jax.ShapeDtypeStruct((rows, part)...  3.29 us
    pallas_call x1, Pallas kernels, finish(): pl.pallas_call(finish_kernel, out_shape=(shape, shape), in_specs=[pl.Bloc...  2.57 us
  transfers between devices with their start and end apart: 1, of which 1 were waited for; matrix products, arithmetic and copies ran while one was open for 0% of the time, Pallas kernels for 3%

profile of v1, /device:TPU:1, one launch (start us, length us, event | category | flops | bytes accessed | tf_op | source)
XLA Modules:
  0.0 98.1 jit_solution(4638233808205403448)
XLA Ops:
  0.6 0.0 copy-start
  0.6 1.3 %copy-done = bf16[2,256,1280]{2,1,0:T(8,128)(2,1)S(1)} copy-done((bf16[2,256,1280]{2,1,0:T(8,128)(2,1)S(1)}, bf16[2,256,1280]{2,1,0:T(8,128)(2,1)}, u32[]{:S(2)}) %copy-start) | copy-done | bytes 1310744
  1.9 0.0 copy-start.2
  2.0 1.3 %copy-done.2 = bf16[2,256,1280]{2,1,0:T(8,128)(2,1)S(1)} copy-done((bf16[2,256,1280]{2,1,0:T(8,128)(2,1)S(1)}, bf16[2,256,1280]{2,1,0:T(8,128)(2,1)}, u32[]{:S(2)}) %copy-start.2) | copy-done | bytes 1310744
  3.3 0.0 copy-start.4
  3.3 1.0 copy-done.4
  4.2 3.3 %route.1 = (bf16[1024,640]{1,0:T(8,128)(2,1)S(1)}, f32[2,256,128]{2,1,0:T(8,128)S(1)}, f32[2,256,128]{2,1,0:T(8,128)S(1)}) custom-call(bf16[2,256,1280]{2,1,0:T(8,128)(2,1)S(1)} %copy-done, bf16[2,256,1280]{2,1,0:T(8,128)(2,1)S(1)} %copy-done.2, bf16[1280,128]{1,0:T(8,128)(2,1)S(1)} %copy-done.4), custom_call_target="tpu_custom_call" | custom-call | tf_op jit(solution)/shard_map/route/pallas_call | solution.py:105
  7.5 33.5 %all_to_all.15 = bf16[128,8,640]{2,1,0:T(8,128)(2,1)S(1)} all-to-all(bf16[128,8,640]{2,1,0:T(8,128)(2,1)S(1)} %bitcast.11), channel_id=1, replica_groups=mesh['group'=4,'member'=32] {'group','member'}, dimensions={0} | all-to-all | bytes 2621440 | tf_op jit(solution)/shard_map/all_to_all | solution.py:292
  41.0 11.5 %expert.1 = bf16[1024,640]{1,0:T(8,128)(2,1)S(1)} custom-call(bf16[1024,640]{1,0:T(8,128)(2,1)S(1)} %bitcast.9, bf16[1,1280,2560]{2,1,0:T(8,128)(2,1)} %refs_1_.1, bf16[1,2560,1280]{2,1,0:T(8,128)(2,1)} %refs_2_.1), custom_call_target="tpu_custom_call" | custom-call | tf_op jit(solution)/shard_map/expert/pallas_call | solution.py:190
  52.5 0.0 copy-start.1
  52.5 0.0 copy-start.3
  52.6 26.2 %all_to_all.16 = bf16[128,8,640]{2,1,0:T(8,128)(2,1)S(1)} all-to-all(bf16[128,8,640]{2,1,0:T(8,128)(2,1)S(1)} %bitcast.10), channel_id=1, replica_groups=mesh['group'=4,'member'=32] {'group','member'}, dimensions={0} | all-to-all | bytes 2621440 | tf_op jit(solution)/shard_map/all_to_all | solution.py:292
  78.8 0.0 copy-done.1
  78.8 0.0 copy-done.3
  78.8 1.5 %logit_grad.1 = (bf16[2,256,128]{2,1,0:T(8,128)(2,1)S(1)}, bf16[256,640]{1,0:T(8,128)(2,1)S(1)}) custom-call(bf16[1024,640]{1,0:T(8,128)(2,1)S(1)} %bitcast.7, bf16[2,256,1280]{2,1,0:T(8,128)(2,1)S(1)} %copy-done.1, bf16[2,256,1280]{2,1,0:T(8,128)(2,1)S(1)} %copy-done.3, f32[2,256,128]{2,1,0:T(8,128)S(1)} %get-tuple-element.11.dispatch, ...), custom_call_target="tpu_custom_call" | custom-call | tf_op jit(solution)/shard_map/logit_grad/pallas_call | solution.py:246
  80.3 0.0 copy-start.5
  80.3 0.8 reshape.29
  81.2 4.3 %all-to-all-start.2 = ((bf16[128,2,640]{2,1,0:T(2,128)(2,1)}), bf16[128,2,640]{2,1,0:T(2,128)(2,1)S(1)}, u32[]{:S(2)}, u32[]{:S(2)}) async-start(bf16[128,2,640]{2,1,0:T(2,128)(2,1)} %reshape.29), calls=%async_computation.2 | async-start | bytes 655360 | tf_op jit(solution)/shard_map/all_to_all | solution.py:292
  85.5 0.0 copy-done.5
  85.5 2.6 %finish.1 = (bf16[2,256,1280]{2,1,0:T(8,128)(2,1)}, bf16[2,256,1280]{2,1,0:T(8,128)(2,1)}) custom-call(bf16[1024,640]{1,0:T(8,128)(2,1)S(1)} %bitcast.8, f32[2,256,128]{2,1,0:T(8,128)S(1)} %get-tuple-element.11.dispatch, f32[2,256,128]{2,1,0:T(8,128)S(1)} %get-tuple-element.12.combine, bf16[2,256,128]{2,1,0:T(8,128)(2,1)S(1)} %get-tuple-element.13.d_logits, ...), custom_call_target="tpu_custom_call" | custom-call | tf_op jit(solution)/shard_map/finish/pallas_call | solution.py:279
  88.0 9.2 %all-to-all-done.2 = bf16[128,2,640]{2,1,0:T(2,128)(2,1)S(1)} async-done(((bf16[128,2,640]{2,1,0:T(2,128)(2,1)}), bf16[128,2,640]{2,1,0:T(2,128)(2,1)S(1)}, u32[]{:S(2)}, u32[]{:S(2)}) %all-to-all-start.2) | async-done | bytes 327712 | tf_op jit(solution)/shard_map/all_to_all | solution.py:292
  97.2 0.3 convert_reduce_fusion
  97.5 0.6 copy.8
Async XLA Ops:
  0.6 1.3 %copy-start = (bf16[2,256,1280]{2,1,0:T(8,128)(2,1)S(1)}, bf16[2,256,1280]{2,1,0:T(8,128)(2,1)}, u32[]{:S(2)}) copy-start(bf16[2,256,1280]{2,1,0:T(8,128)(2,1)} %tokens.1) | copy-start | bytes 3932164
  1.9 1.3 %copy-start.2 = (bf16[2,256,1280]{2,1,0:T(8,128)(2,1)S(1)}, bf16[2,256,1280]{2,1,0:T(8,128)(2,1)}, u32[]{:S(2)}) copy-start(bf16[2,256,1280]{2,1,0:T(8,128)(2,1)} %upstream.1) | copy-start | bytes 3932164
  3.3 1.0 copy-start.4
  52.5 26.2 %copy-start.1 = (bf16[2,256,1280]{2,1,0:T(8,128)(2,1)S(1)}, bf16[2,256,1280]{2,1,0:T(8,128)(2,1)}, u32[]{:S(2)}) copy-start(bf16[2,256,1280]{2,1,0:T(8,128)(2,1)} %tokens.1) | copy-start | bytes 3932164
  52.5 26.2 %copy-start.3 = (bf16[2,256,1280]{2,1,0:T(8,128)(2,1)S(1)}, bf16[2,256,1280]{2,1,0:T(8,128)(2,1)}, u32[]{:S(2)}) copy-start(bf16[2,256,1280]{2,1,0:T(8,128)(2,1)} %upstream.1) | copy-start | bytes 3932164
  80.3 5.2 %copy-start.5 = (bf16[1280,128]{1,0:T(8,128)(2,1)S(1)}, bf16[1280,128]{1,0:T(8,128)(2,1)}, u32[]{:S(2)}) copy-start(bf16[1280,128]{1,0:T(8,128)(2,1)} %key.1) | copy-start | bytes 983044
  81.2 16.1 %all-to-all-start.2 = ((bf16[128,2,640]{2,1,0:T(2,128)(2,1)}), bf16[128,2,640]{2,1,0:T(2,128)(2,1)S(1)}, u32[]{:S(2)}, u32[]{:S(2)}) async-start(bf16[128,2,640]{2,1,0:T(2,128)(2,1)} %reshape.29), calls=%async_computation.2 | async-start | bytes 655360 | tf_op jit(solution)/shard_map/all_to_all | solution.py:292

commit v2 on v1

--- a/solution.py
+++ b/solution.py
@@ -8,9 +8,10 @@
 AXES = ("group", "member")
 HALVES = 2
 LANES = 128
+LOAD_PARTS = 1
 KINDS = 2
-CHUNK = 512
-VMEM_LIMIT = 48 * 1024 * 1024
+VMEM_LIMIT = 16 * 1024 * 1024
+EXPERT_VMEM = 28 * 1024 * 1024
 GELU_SCALE = 0.7978845608028654
 GELU_CUBIC = 0.044715
 
@@ -109,7 +110,7 @@
             jax.ShapeDtypeStruct((images, patches, slots), jnp.float32),
             jax.ShapeDtypeStruct((images, patches, slots), jnp.float32),
         ),
-        in_specs=[pl.BlockSpec(memory_space=pl.ANY)] * 3,
+        in_specs=[pl.BlockSpec(memory_space=pltpu.HBM)] * 3,
         out_specs=(pl.BlockSpec(memory_space=pltpu.VMEM),) * 3,
         scratch_shapes=[
             pltpu.VMEM(tokens.shape, tokens.dtype),
@@ -120,99 +121,89 @@
         ],
         compiler_params=pltpu.CompilerParams(vmem_limit_bytes=VMEM_LIMIT),
         name="route",
-    )(tokens, upstream, slot_key_matrix)
-
-
-def expert_kernel(
-    images, arrived, w_in_hbm, w_out_hbm, sent, w_in, w_out, spread, rows_in, rows_grad, out, back, sems
-):
-    steps, width, chunk = w_in.shape
+    )(*(pltpu.with_memory_space_constraint(x, pltpu.HBM) for x in (tokens, upstream, slot_key_matrix)))
+
+
+def hold_kernel(rows, out):
+    del rows, out
+
+
+def hold(rows):
+    return pl.pallas_call(
+        hold_kernel,
+        out_shape=jax.ShapeDtypeStruct(rows.shape, rows.dtype),
+        in_specs=[pl.BlockSpec(memory_space=pl.ANY)],
+        out_specs=pl.BlockSpec(memory_space=pl.ANY),
+        input_output_aliases={0: 0},
+        cost_estimate=pl.CostEstimate(flops=10**9, bytes_accessed=10**8, transcendentals=10**6),
+        compiler_params=pltpu.CompilerParams(vmem_limit_bytes=1024 * 1024),
+        name="hold",
+    )(rows)
+
+
+def expert_kernel(images, arrived, w_in, w_out_hbm, sent, w_out, spread, answers, sems):
     peers = arrived.shape[0] // (KINDS * images * HALVES)
-
-    def weight_copies(step):
-        at = pl.multiple_of(step * chunk, chunk)
-        return (
-            pltpu.make_async_copy(
-                w_in_hbm.at[0, :, pl.ds(at, chunk)], w_in.at[step], sems.at[0, step]
-            ),
-            pltpu.make_async_copy(
-                w_out_hbm.at[0, pl.ds(at, chunk), :], w_out.at[step], sems.at[1, step]
-            ),
+    hidden = w_out.shape[0] // LOAD_PARTS
+    copies = []
+    for at in range(LOAD_PARTS):
+        part = pl.ds(at * hidden, hidden)
+        copies.append(pltpu.make_async_copy(w_out_hbm.at[0, part], w_out.at[part], sems.at[at]))
+    for copy in copies:
+        copy.start()
+    widen(spread, arrived)
+
+    def rows_of(kind):
+        return jnp.concatenate(
+            [pick(spread, kind, image, images, peers) for image in range(images)], axis=0
         )
 
-    def begin(step, carry):
-        for copy in weight_copies(step):
-            copy.start()
-        return carry
-
-    lax.fori_loop(0, steps, begin, 0)
-    widen(spread, arrived)
-    for image in range(images):
-        rows = pl.ds(image * peers, peers)
-        rows_in[rows, :] = pick(spread, 0, image, images, peers)
-        rows_grad[rows, :] = pick(spread, 1, image, images, peers)
-    out[...] = jnp.zeros_like(out)
-    back[...] = jnp.zeros_like(back)
-
-    def one(step, carry):
-        for copy in weight_copies(step):
-            copy.wait()
-        pre = row_dot(rows_in[...], w_in[step])
-        square = pre * pre
-        tanh = jnp.tanh(GELU_SCALE * (pre * (1.0 + GELU_CUBIC * square)))
-        gate = 0.5 * (1.0 + tanh)
-        activated = (pre * gate).astype(jnp.bfloat16)
-        slope = gate + 0.5 * pre * (1.0 - tanh * tanh) * (
-            GELU_SCALE * (1.0 + 3.0 * GELU_CUBIC * square)
-        )
-        out[...] += row_dot(activated, w_out[step])
-        d_act = row_dot_t(rows_grad[...], w_out[step])
-        d_pre = (d_act * slope).astype(jnp.bfloat16)
-        back[...] += row_dot_t(d_pre, w_in[step])
-        return carry
-
-    lax.fori_loop(0, steps, one, 0)
-    for image in range(images):
-        rows = pl.ds(image * peers, peers)
-        place(spread, 0, image, images, out[rows, :])
-        place(spread, 1, image, images, back[rows, :])
-    narrow(sent, spread)
+    def answer(kind, rows):
+        for image in range(images):
+            place(answers, kind, image, images, rows[image * peers : (image + 1) * peers])
+
+    pre = row_dot(rows_of(0), w_in[0])
+    rows_grad = rows_of(1)
+    d_act = []
+    for at, copy in enumerate(copies):
+        copy.wait()
+        d_act.append(row_dot_t(rows_grad, w_out[at * hidden : (at + 1) * hidden]))
+    d_act = jnp.concatenate(d_act, axis=1)
+    square = pre * pre
+    tanh = jnp.tanh(GELU_SCALE * (pre * (1.0 + GELU_CUBIC * square)))
+    gate = 0.5 * (1.0 + tanh)
+    activated = (pre * gate).astype(jnp.bfloat16)
+    slope = gate + 0.5 * pre * (1.0 - tanh * tanh) * (
+        GELU_SCALE * (1.0 + 3.0 * GELU_CUBIC * square)
+    )
+    d_pre = (d_act * slope).astype(jnp.bfloat16)
+    answer(0, row_dot(activated, w_out[...]))
+    answer(1, row_dot_t(d_pre, w_in[0]))
+    narrow(sent, answers)
 
 
 def expert(arrived, w_in, w_out, images):
-    _, width, hidden = w_in.shape
-    steps = hidden // CHUNK
-    rows = arrived.shape[0] // (KINDS * HALVES)
-
     def body(*refs):
         expert_kernel(images, *refs)
 
     return pl.pallas_call(
         body,
         out_shape=jax.ShapeDtypeStruct(arrived.shape, jnp.bfloat16),
-        in_specs=[
-            pl.BlockSpec(memory_space=pltpu.VMEM),
-            pl.BlockSpec(memory_space=pl.ANY),
-            pl.BlockSpec(memory_space=pl.ANY),
-        ],
+        in_specs=[pl.BlockSpec(memory_space=pltpu.VMEM)] * 2
+        + [pl.BlockSpec(memory_space=pltpu.HBM)],
         out_specs=pl.BlockSpec(memory_space=pltpu.VMEM),
         scratch_shapes=[
-            pltpu.VMEM((steps, width, CHUNK), w_in.dtype),
-            pltpu.VMEM((steps, CHUNK, width), w_out.dtype),
+            pltpu.VMEM(w_out.shape[1:], w_out.dtype),
             spread_shape(*arrived.shape),
-            pltpu.VMEM((rows, width), jnp.bfloat16),
-            pltpu.VMEM((rows, width), jnp.bfloat16),
-            pltpu.VMEM((rows, width), jnp.float32),
-            pltpu.VMEM((rows, width), jnp.float32),
-            pltpu.SemaphoreType.DMA((2, steps)),
+            spread_shape(*arrived.shape),
+            pltpu.SemaphoreType.DMA((LOAD_PARTS,)),
         ],
-        compiler_params=pltpu.CompilerParams(vmem_limit_bytes=VMEM_LIMIT),
+        compiler_params=pltpu.CompilerParams(vmem_limit_bytes=EXPERT_VMEM),
         name="expert",
-    )(arrived, w_in, w_out)
+    )(arrived, w_in, pltpu.with_memory_space_constraint(w_out, pltpu.HBM))
 
 
 def logit_grad_kernel(
-    arrived, tokens, upstream, dispatch, combine, d_logits, key_part, spread, spread_key
+    arrived, tokens, upstream, dispatch, combine, d_logits, key_part, spread
 ):
     images, patches, width = tokens.shape
     slots = dispatch.shape[2]
@@ -230,19 +221,16 @@
         both = both.astype(jnp.bfloat16)
         d_logits[image] = both
         total += col_dot(both, tokens[image])
-    lane_blocks = spread_key.shape[0]
+    part = width // HALVES
     for half in range(HALVES):
-        for block in range(lane_blocks):
-            first = (half * lane_blocks + block) * LANES
-            lanes = total[:, first : first + LANES]
-            spread_key[block, pl.ds(half, slots, stride=HALVES), :] = lanes
-    narrow(key_part, spread_key)
+        lanes = total[:, half * part : (half + 1) * part]
+        key_part[:, half, :] = lanes.astype(jnp.bfloat16)
 
 
 def logit_grad(arrived, tokens, upstream, dispatch, combine):
     images, patches, width = tokens.shape
     slots = dispatch.shape[2]
-    key_shape = (slots * HALVES, width // HALVES)
+    key_shape = (slots, HALVES, width // HALVES)
     return pl.pallas_call(
         logit_grad_kernel,
         out_shape=(
@@ -251,10 +239,7 @@
         ),
         in_specs=[pl.BlockSpec(memory_space=pltpu.VMEM)] * 5,
         out_specs=(pl.BlockSpec(memory_space=pltpu.VMEM),) * 2,
-        scratch_shapes=[
-            spread_shape(*arrived.shape),
-            spread_shape(*key_shape),
-        ],
+        scratch_shapes=[spread_shape(*arrived.shape)],
         compiler_params=pltpu.CompilerParams(vmem_limit_bytes=VMEM_LIMIT),
         name="logit_grad",
     )(arrived, tokens, upstream, dispatch, combine)
@@ -287,23 +272,43 @@
     )(arrived, dispatch, combine, d_logits, slot_key_matrix)
 
 
-def exchange(rows, peers):
-    blocks = rows.reshape(peers, -1, rows.shape[1])
-    blocks = lax.all_to_all(blocks, AXES, split_axis=0, concat_axis=0, tiled=True)
-    return blocks.reshape(rows.shape)
+def key_sum_kernel(terms, total):
+    part = terms.shape[2]
+    own = jnp.sum(terms[...].astype(jnp.float32), axis=0)
+    for half in range(HALVES):
+        total[:, half * part : (half + 1) * part] = own[half : half + 1]
+
+
+def key_sum(terms):
+    return pl.pallas_call(
+        key_sum_kernel,
+        out_shape=jax.ShapeDtypeStruct((1, terms.shape[1] * terms.shape[2]), jnp.float32),
+        in_specs=[pl.BlockSpec(memory_space=pltpu.VMEM)],
+        out_specs=pl.BlockSpec(memory_space=pltpu.VMEM),
+        compiler_params=pltpu.CompilerParams(vmem_limit_bytes=VMEM_LIMIT),
+        name="key_sum",
+    )(terms)
+
+
+def exchange(blocks):
+    return lax.all_to_all(blocks, AXES, split_axis=0, concat_axis=0, tiled=True)
+
+
+def exchange_rows(rows, peers):
+    return exchange(rows.reshape(peers, -1, rows.shape[1])).reshape(rows.shape)
 
 
 def shards(tokens, slot_key_matrix, w_in, w_out, upstream):
     images, patches, width = tokens.shape
     slots = slot_key_matrix.shape[1]
     sent, dispatch, combine = route(tokens, upstream, slot_key_matrix)
-    arrived = exchange(sent, slots)
+    arrived = exchange_rows(hold(sent), slots)
     answered = expert(arrived, w_in, w_out, images)
-    returned = exchange(answered, slots)
+    returned = exchange_rows(answered, slots)
     d_logits, key_part = logit_grad(returned, tokens, upstream, dispatch, combine)
-    key_terms = exchange(key_part, slots)
+    key_terms = exchange(key_part)
     mixed, token_grad = finish(returned, dispatch, combine, d_logits, slot_key_matrix)
-    key_grad = jnp.sum(key_terms.reshape(slots, 1, width).astype(jnp.float32), axis=0)
+    key_grad = key_sum(key_terms)
     return (mixed, token_grad, key_grad)
 
 

time: 98.4 us -> 92.5 us (0.940)
  local copies, waits for them, and re-layouts: 5.06 us -> 0.02 us
    unnamed x13 -> x8, local copies, waits for them, and re-layouts: 4.22 us -> 0.02 us
    pallas_call x1, Pallas kernels: 11.5 us -> 8.85 us  [expert(): pl.pallas_call(body, out_shape=jax.ShapeDtypeStruct(arrived.shape, jnp.bf...]
where the time goes in v2:
time: 92.5 us; the launch traced here: 92.3 us
  blocking collectives  59.7 us (65%)
  Pallas kernels  18.4 us (20%)
  waiting for transfers between devices  9.18 us (10%)
  starting transfers between devices  4.29 us (5%)
    all_to_all x2, blocking collectives, exchange(): return lax.all_to_all(blocks, AXES, split_axis=0, concat_axis=0, tiled=True)  59.7 us
    all_to_all x1, waiting for transfers between devices, exchange(): return lax.all_to_all(blocks, AXES, split_axis=0, concat_axis=0, tiled=True)  9.18 us
    pallas_call x1, Pallas kernels, expert(): pl.pallas_call(body, out_shape=jax.ShapeDtypeStruct(arrived.shape, jnp.bf...  8.85 us
    all_to_all x1, starting transfers between devices, exchange(): return lax.all_to_all(blocks, AXES, split_axis=0, concat_axis=0, tiled=True)  4.29 us
    pallas_call x1, Pallas kernels, route(): pl.pallas_call(route_kernel, out_shape=(jax.ShapeDtypeStruct((rows, part)...  3.7 us
    pallas_call x1, Pallas kernels, finish(): pl.pallas_call(finish_kernel, out_shape=(shape, shape), in_specs=[pl.Bloc...  2.57 us
    pallas_call x1, Pallas kernels, logit_grad(): pl.pallas_call(logit_grad_kernel, out_shape=(jax.ShapeDtypeStruct(dispatc...  2.31 us
  transfers between devices with their start and end apart: 1, of which 1 were waited for; matrix products, arithmetic and copies ran while one was open for 0% of the time, Pallas kernels for 3%

profile of v2, /device:TPU:1, one launch (start us, length us, event | category | flops | bytes accessed | tf_op | source)
XLA Modules:
  0.0 92.3 jit_solution(7423613848136888762)
XLA Ops:
  0.6 0.0 copy-start
  0.6 3.7 %route.1 = (bf16[1024,640]{1,0:T(8,128)(2,1)S(1)}, f32[2,256,128]{2,1,0:T(8,128)S(1)}, f32[2,256,128]{2,1,0:T(8,128)S(1)}) custom-call(bf16[2,256,1280]{2,1,0:T(8,128)(2,1)} %tokens.1, bf16[2,256,1280]{2,1,0:T(8,128)(2,1)} %upstream.1, bf16[1280,128]{1,0:T(8,128)(2,1)} %key.1), custom_call_target="tpu_custom_call" | custom-call | tf_op jit(solution)/shard_map/route/pallas_call | solution.py:106
  4.4 33.5 %all_to_all.15 = bf16[128,8,640]{2,1,0:T(8,128)(2,1)S(1)} all-to-all(bf16[128,8,640]{2,1,0:T(8,128)(2,1)S(1)} %bitcast.8), channel_id=1, replica_groups=mesh['group'=4,'member'=32] {'group','member'}, dimensions={0} | all-to-all | bytes 2621440 | tf_op jit(solution)/shard_map/all_to_all | solution.py:294
  37.8 0.0 copy-done
  37.8 8.9 %expert.1 = bf16[1024,640]{1,0:T(8,128)(2,1)S(1)} custom-call(bf16[1024,640]{1,0:T(8,128)(2,1)S(1)} %bitcast.6, bf16[1,1280,2560]{2,1,0:T(8,128)(2,1)S(1)} %copy-done, bf16[1,2560,1280]{2,1,0:T(8,128)(2,1)} %refs_2_.1), custom_call_target="tpu_custom_call" | custom-call | tf_op jit(solution)/shard_map/expert/pallas_call | solution.py:188
  46.7 0.0 copy-start.1
  46.7 0.0 copy-start.2
  46.7 26.2 %all_to_all.16 = bf16[128,8,640]{2,1,0:T(8,128)(2,1)S(1)} all-to-all(bf16[128,8,640]{2,1,0:T(8,128)(2,1)S(1)} %bitcast.7), channel_id=1, replica_groups=mesh['group'=4,'member'=32] {'group','member'}, dimensions={0} | all-to-all | bytes 2621440 | tf_op jit(solution)/shard_map/all_to_all | solution.py:294
  72.9 0.0 copy-done.1
  72.9 0.0 copy-done.2
  72.9 0.0 copy-start.3
  72.9 2.3 %logit_grad.1 = (bf16[2,256,128]{2,1,0:T(8,128)(2,1)S(1)}, bf16[128,2,640]{2,1,0:T(2,128)(2,1)}) custom-call(bf16[1024,640]{1,0:T(8,128)(2,1)S(1)} %bitcast.4, bf16[2,256,1280]{2,1,0:T(8,128)(2,1)S(1)} %copy-done.1, bf16[2,256,1280]{2,1,0:T(8,128)(2,1)S(1)} %copy-done.2, f32[2,256,128]{2,1,0:T(8,128)S(1)} %get-tuple-element.11.dispatch, ...), custom_call_target="tpu_custom_call" | custom-call | tf_op jit(solution)/shard_map/logit_grad/pallas_call | solution.py:234
  75.2 4.3 %all-to-all-start.2 = ((bf16[128,2,640]{2,1,0:T(2,128)(2,1)}), bf16[128,2,640]{2,1,0:T(2,128)(2,1)S(1)}, u32[]{:S(2)}, u32[]{:S(2)}) async-start(bf16[128,2,640]{2,1,0:T(2,128)(2,1)} %get-tuple-element.16), calls=%async_computation.2 | async-start | bytes 655360 | tf_op jit(solution)/shard_map/all_to_all | solution.py:294
  79.5 0.0 copy-done.3
  79.5 2.6 %finish.1 = (bf16[2,256,1280]{2,1,0:T(8,128)(2,1)}, bf16[2,256,1280]{2,1,0:T(8,128)(2,1)}) custom-call(bf16[1024,640]{1,0:T(8,128)(2,1)S(1)} %bitcast.5, f32[2,256,128]{2,1,0:T(8,128)S(1)} %get-tuple-element.11.dispatch, f32[2,256,128]{2,1,0:T(8,128)S(1)} %get-tuple-element.12.combine, bf16[2,256,128]{2,1,0:T(8,128)(2,1)S(1)} %get-tuple-element.13.d_logits, ...), custom_call_target="tpu_custom_call" | custom-call | tf_op jit(solution)/shard_map/finish/pallas_call | solution.py:264
  82.1 9.2 %all-to-all-done.2.terms = bf16[128,2,640]{2,1,0:T(2,128)(2,1)S(1)} async-done(((bf16[128,2,640]{2,1,0:T(2,128)(2,1)}), bf16[128,2,640]{2,1,0:T(2,128)(2,1)S(1)}, u32[]{:S(2)}, u32[]{:S(2)}) %all-to-all-start.2) | async-done | bytes 327712 | tf_op jit(solution)/shard_map/all_to_all | solution.py:294
  91.3 1.0 %key_sum.1 = f32[1,1280]{1,0:T(1,128)} custom-call(bf16[128,2,640]{2,1,0:T(2,128)(2,1)S(1)} %all-to-all-done.2.terms), custom_call_target="tpu_custom_call" | custom-call | tf_op jit(solution)/shard_map/key_sum/pallas_call | solution.py:283
  (1 shorter events, 0.0 us)
Async XLA Ops:
  0.6 37.2 %copy-start = (bf16[1,1280,2560]{2,1,0:T(8,128)(2,1)S(1)}, bf16[1,1280,2560]{2,1,0:T(8,128)(2,1)}, u32[]{:S(2)}) copy-start(bf16[1,1280,2560]{2,1,0:T(8,128)(2,1)} %refs_1_.1) | copy-start | bytes 19660804
  46.7 26.2 %copy-start.1 = (bf16[2,256,1280]{2,1,0:T(8,128)(2,1)S(1)}, bf16[2,256,1280]{2,1,0:T(8,128)(2,1)}, u32[]{:S(2)}) copy-start(bf16[2,256,1280]{2,1,0:T(8,128)(2,1)} %tokens.1) | copy-start | bytes 3932164
  46.7 26.2 %copy-start.2 = (bf16[2,256,1280]{2,1,0:T(8,128)(2,1)S(1)}, bf16[2,256,1280]{2,1,0:T(8,128)(2,1)}, u32[]{:S(2)}) copy-start(bf16[2,256,1280]{2,1,0:T(8,128)(2,1)} %upstream.1) | copy-start | bytes 3932164
  72.9 6.6 %copy-start.3 = (bf16[1280,128]{1,0:T(8,128)(2,1)S(1)}, bf16[1280,128]{1,0:T(8,128)(2,1)}, u32[]{:S(2)}) copy-start(bf16[1280,128]{1,0:T(8,128)(2,1)} %key.1) | copy-start | bytes 983044
  75.2 16.1 %all-to-all-start.2 = ((bf16[128,2,640]{2,1,0:T(2,128)(2,1)}), bf16[128,2,640]{2,1,0:T(2,128)(2,1)S(1)}, u32[]{:S(2)}, u32[]{:S(2)}) async-start(bf16[128,2,640]{2,1,0:T(2,128)(2,1)} %get-tuple-element.16), calls=%async_computation.2 | async-start | bytes 655360 | tf_op jit(solution)/shard_map/all_to_all | solution.py:294

commit v3 on v2

v3 whole, which is shorter than its diff:
```python
import functools
import math

import jax
import jax.numpy as jnp
from jax import lax
from jax.experimental import pallas as pl
from jax.experimental.pallas import tpu as pltpu
from jax.sharding import PartitionSpec as P

AXES = ("group", "member")
EXCHANGE_AXES = ("member", "group")
HALVES = 2
LANES = 128
KINDS = 2
VMEM_LIMIT = 16 * 1024 * 1024
EXPERT_VMEM = 28 * 1024 * 1024
GELU_SCALE = 0.7978845608028654
GELU_CUBIC = 0.044715


def row_dot(a, b):
    return lax.dot_general(a, b, (((1,), (0,)), ((), ())), preferred_element_type=jnp.float32)


def row_dot_t(a, b):
    return lax.dot_general(a, b, (((1,), (1,)), ((), ())), preferred_element_type=jnp.float32)


def col_dot(a, b):
    return lax.dot_general(a, b, (((0,), (0,)), ((), ())), preferred_element_type=jnp.float32)


def place(spread, kind, image, images, rows):
    peers, width = rows.shape
    per_peer = KINDS * images * HALVES
    lane_blocks = spread.shape[0]
    for half in range(HALVES):
        at = (kind * images + image) * HALVES + half
        for block in range(lane_blocks):
            first = (half * lane_blocks + block) * LANES
            spread[block, pl.ds(at, peers, stride=per_peer), :] = rows[:, first : first + LANES]


def pick(spread, kind, image, images, peers):
    per_peer = KINDS * images * HALVES
    parts = []
    for half in range(HALVES):
        at = (kind * images + image) * HALVES + half
        for block in range(spread.shape[0]):
            rows = spread[block, pl.ds(at, peers, stride=per_peer), :]
            parts.append(rows.astype(jnp.bfloat16))
    return jnp.concatenate(parts, axis=1)


def widen(spread, arrived, groups):
    rows = spread.shape[1] // groups
    for block in range(spread.shape[0]):
        lanes = slice(block * LANES, (block + 1) * LANES)
        for group in range(groups):
            own = arrived[:, group, :, lanes].astype(jnp.float32)
            spread[block, group * rows : (group + 1) * rows, :] = own.reshape(rows, LANES)


def narrow(sent, spread, groups):
    rows = spread.shape[1] // groups
    per_peer = sent.shape[2]
    for block in range(spread.shape[0]):
        lanes = slice(block * LANES, (block + 1) * LANES)
        for group in range(groups):
            own = spread[block, group * rows : (group + 1) * rows, :]
            sent[:, group, :, lanes] = own.reshape(-1, per_peer, LANES).astype(jnp.bfloat16)


def spread_shape(rows, part):
    return pltpu.VMEM((part // LANES, rows, LANES), jnp.float32)


def route_kernel(
    groups,
    tokens_hbm,
    upstream_hbm,
    key_hbm,
    weight_hbm,
    sent,
    dispatch,
    combine,
    weight,
    tokens,
    upstream,
    key,
    spread,
    sems,
):
    images = tokens.shape[0]
    key_copy = pltpu.make_async_copy(key_hbm, key, sems.at[2 * images])
    key_copy.start()
    copies = []
    for place_at, (source, target) in enumerate(((tokens_hbm, tokens), (upstream_hbm, upstream))):
        for image in range(images):
            copy = pltpu.make_async_copy(
                source.at[image], target.at[image], sems.at[2 * image + place_at]
            )
            copy.start()
            copies.append(copy)
    weight_copy = pltpu.make_async_copy(weight_hbm.at[0], weight, sems.at[2 * images + 1])
    weight_copy.start()
    key_copy.wait()
    for image in range(images):
        copies[image].wait()
    slot_weights = []
    for image in range(images):
        logits = row_dot(tokens[image], key[...])
        by_token = jnp.exp(logits - jnp.max(logits, axis=0, keepdims=True))
        by_token = by_token / jnp.sum(by_token, axis=0, keepdims=True)
        dispatch[image] = by_token
        by_slot = jnp.exp(logits - jnp.max(logits, axis=1, keepdims=True))
        by_slot = by_slot / jnp.sum(by_slot, axis=1, keepdims=True)
        combine[image] = by_slot
        slot_weights.append(by_slot.astype(jnp.bfloat16))
        slot_in = col_dot(by_token.astype(jnp.bfloat16), tokens[image])
        place(spread, 0, image, images, slot_in)
    for image in range(images):
        copies[images + image].wait()
    for image in range(images):
        d_slot_out = col_dot(slot_weights[image], upstream[image])
        place(spread, 1, image, images, d_slot_out)
    narrow(sent, spread, groups)
    weight_copy.wait()


def route(tokens, upstream, slot_key_matrix, weight, groups):
    images, patches, width = tokens.shape
    slots = slot_key_matrix.shape[1]
    per_peer = KINDS * images * HALVES
    rows = slots * per_peer
    part = width // HALVES
    return pl.pallas_call(
        functools.partial(route_kernel, groups),
        out_shape=(
            jax.ShapeDtypeStruct((slots // groups, groups, per_peer, part), jnp.bfloat16),
            jax.ShapeDtypeStruct((images, patches, slots), jnp.float32),
            jax.ShapeDtypeStruct((images, patches, slots), jnp.float32),
            pltpu.VMEM(weight.shape[1:], weight.dtype),
        ),
        in_specs=[pl.BlockSpec(memory_space=pltpu.HBM)] * 4,
        out_specs=(pl.BlockSpec(memory_space=pltpu.VMEM),) * 4,
        scratch_shapes=[
            pltpu.VMEM(tokens.shape, tokens.dtype),
            pltpu.VMEM(upstream.shape, upstream.dtype),
            pltpu.VMEM(slot_key_matrix.shape, slot_key_matrix.dtype),
            spread_shape(rows, part),
            pltpu.SemaphoreType.DMA((2 * images + 2,)),
        ],
        compiler_params=pltpu.CompilerParams(vmem_limit_bytes=VMEM_LIMIT),
        name="route",
    )(*(pltpu.with_memory_space_constraint(x, pltpu.HBM) for x in (tokens, upstream, slot_key_matrix, weight)))


def hold_kernel(rows, out):
    del rows, out


def hold(rows):
    return pl.pallas_call(
        hold_kernel,
        out_shape=jax.ShapeDtypeStruct(rows.shape, rows.dtype),
        in_specs=[pl.BlockSpec(memory_space=pl.ANY)],
        out_specs=pl.BlockSpec(memory_space=pl.ANY),
        input_output_aliases={0: 0},
        cost_estimate=pl.CostEstimate(flops=10**9, bytes_accessed=10**8, transcendentals=10**6),
        compiler_params=pltpu.CompilerParams(vmem_limit_bytes=1024 * 1024),
        name="hold",
    )(rows)


def expert_kernel(images, arrived, w_in, w_out, sent, spread, answers):
    peers = arrived.shape[0] // (KINDS * images * HALVES)
    for block in range(spread.shape[0]):
        lanes = slice(block * LANES, (block + 1) * LANES)
        spread[block] = arrived[:, lanes].astype(jnp.float32)

    def rows_of(kind):
        return jnp.concatenate(
            [pick(spread, kind, image, images, peers) for image in range(images)], axis=0
        )

    def answer(kind, rows):
        for image in range(images):
            place(answers, kind, image, images, rows[image * peers : (image + 1) * peers])

    pre = row_dot(rows_of(0), w_in[0])
    square = pre * pre
    tanh = jnp.tanh(GELU_SCALE * (pre * (1.0 + GELU_CUBIC * square)))
    gate = 0.5 * (1.0 + tanh)
    activated = (pre * gate).astype(jnp.bfloat16)
    slope = gate + 0.5 * pre * (1.0 - tanh * tanh) * (
        GELU_SCALE * (1.0 + 3.0 * GELU_CUBIC * square)
    )
    d_act = row_dot_t(rows_of(1), w_out[...])
    d_pre = (d_act * slope).astype(jnp.bfloat16)
    answer(0, row_dot(activated, w_out[...]))
    answer(1, row_dot_t(d_pre, w_in[0]))
    for block in range(spread.shape[0]):
        lanes = slice(block * LANES, (block + 1) * LANES)
        sent[:, lanes] = answers[block].astype(jnp.bfloat16)


def expert(arrived, w_in, w_out, images):
    def body(*refs):
        expert_kernel(images, *refs)

    return pl.pallas_call(
        body,
        out_shape=jax.ShapeDtypeStruct(arrived.shape, jnp.bfloat16),
        in_specs=[pl.BlockSpec(memory_space=pltpu.VMEM)] * 3,
        out_specs=pl.BlockSpec(memory_space=pltpu.VMEM),
        scratch_shapes=[spread_shape(*arrived.shape), spread_shape(*arrived.shape)],
        compiler_params=pltpu.CompilerParams(vmem_limit_bytes=EXPERT_VMEM),
        name="expert",
    )(arrived, w_in, w_out)


def logit_grad_kernel(
    groups, arrived, tokens, upstream, dispatch, combine, d_logits, key_part, spread
):
    images, patches, width = tokens.shape
    slots = dispatch.shape[2]
    widen(spread, arrived, groups)
    total = jnp.zeros((slots, width), jnp.float32)
    for image in range(images):
        returned = pick(spread, 0, image, images, slots)
        d_slot_in = pick(spread, 1, image, images, slots)
        d_combine = row_dot_t(upstream[image], returned)
        by_slot = combine[image]
        both = by_slot * (d_combine - jnp.sum(by_slot * d_combine, axis=1, keepdims=True))
        d_dispatch = row_dot_t(tokens[image], d_slot_in)
        by_token = dispatch[image]
        both += by_token * (d_dispatch - jnp.sum(by_token * d_dispatch, axis=0, keepdims=True))
        both = both.astype(jnp.bfloat16)
        d_logits[image] = both
        total += col_dot(both, tokens[image])
    part = width // HALVES
    members = slots // groups
    for half in range(HALVES):
        lanes = total[:, half * part : (half + 1) * part]
        for group in range(groups):
            rows = lanes[group * members : (group + 1) * members]
            key_part[:, group, half, :] = rows.astype(jnp.bfloat16)


def logit_grad(arrived, tokens, upstream, dispatch, combine, groups):
    images, patches, width = tokens.shape
    slots = dispatch.shape[2]
    key_shape = (slots // groups, groups, HALVES, width // HALVES)
    return pl.pallas_call(
        functools.partial(logit_grad_kernel, groups),
        out_shape=(
            jax.ShapeDtypeStruct(dispatch.shape, jnp.bfloat16),
            jax.ShapeDtypeStruct(key_shape, jnp.bfloat16),
        ),
        in_specs=[pl.BlockSpec(memory_space=pltpu.VMEM)] * 5,
        out_specs=(pl.BlockSpec(memory_space=pltpu.VMEM),) * 2,
        scratch_shapes=[spread_shape(math.prod(arrived.shape[:-1]), arrived.shape[-1])],
        compiler_params=pltpu.CompilerParams(vmem_limit_bytes=VMEM_LIMIT),
        name="logit_grad",
    )(arrived, tokens, upstream, dispatch, combine)


def finish_kernel(groups, arrived, dispatch, combine, d_logits, key, mixed, token_grad, spread):
    images, patches, slots = dispatch.shape
    widen(spread, arrived, groups)
    for image in range(images):
        returned = pick(spread, 0, image, images, slots)
        mixed[image] = row_dot(combine[image].astype(jnp.bfloat16), returned).astype(jnp.bfloat16)
        d_slot_in = pick(spread, 1, image, images, slots)
        grad = row_dot_t(d_logits[image], key[...])
        grad += row_dot(dispatch[image].astype(jnp.bfloat16), d_slot_in)
        token_grad[image] = grad.astype(jnp.bfloat16)


def finish(arrived, dispatch, combine, d_logits, slot_key_matrix, groups):
    images, patches, slots = dispatch.shape
    width = slot_key_matrix.shape[0]
    shape = jax.ShapeDtypeStruct((images, patches, width), jnp.bfloat16)
    return pl.pallas_call(
        functools.partial(finish_kernel, groups),
        out_shape=(shape, shape),
        in_specs=[pl.BlockSpec(memory_space=pltpu.VMEM)] * 5,
        out_specs=(pl.BlockSpec(memory_space=pltpu.VMEM),) * 2,
        scratch_shapes=[spread_shape(math.prod(arrived.shape[:-1]), arrived.shape[-1])],
        compiler_params=pltpu.CompilerParams(vmem_limit_bytes=VMEM_LIMIT),
        name="finish",
    )(arrived, dispatch, combine, d_logits, slot_key_matrix)


def key_sum_kernel(terms, total):
    part = terms.shape[2]
    own = jnp.sum(terms[...].astype(jnp.float32), axis=0)
    for half in range(HALVES):
        total[:, half * part : (half + 1) * part] = own[half : half + 1]


def key_sum(terms):
    return pl.pallas_call(
        key_sum_kernel,
        out_shape=jax.ShapeDtypeStruct((1, terms.shape[1] * terms.shape[2]), jnp.float32),
        in_specs=[pl.BlockSpec(memory_space=pltpu.VMEM)],
        out_specs=pl.BlockSpec(memory_space=pltpu.VMEM),
        compiler_params=pltpu.CompilerParams(vmem_limit_bytes=VMEM_LIMIT),
        name="key_sum",
    )(terms)


def exchange(blocks):
    return lax.all_to_all(blocks, EXCHANGE_AXES, split_axis=0, concat_axis=0, tiled=True)


def shards(tokens, slot_key_matrix, w_in, w_out, upstream, groups=4):
    images, patches, width = tokens.shape
    slots = slot_key_matrix.shape[1]
    sent, dispatch, combine, w_out = route(tokens, upstream, slot_key_matrix, w_out, groups)
    by_group = sent.shape
    per_peer, part = by_group[2:]
    arrived = exchange(hold(sent).reshape(slots, per_peer, part))
    answered = expert(arrived.reshape(-1, part), w_in, w_out, images)
    returned = exchange(answered.reshape(slots, per_peer, part)).reshape(by_group)
    d_logits, key_part = logit_grad(returned, tokens, upstream, dispatch, combine, groups)
    key_terms = exchange(key_part.reshape(slots, HALVES, -1))
    mixed, token_grad = finish(returned, dispatch, combine, d_logits, slot_key_matrix, groups)
    key_grad = key_sum(key_terms)
    return (mixed, token_grad, key_grad)


def solution(mesh):
    in_specs = (
        P(AXES, None, None),
        P(),
        P(AXES, None, None),
        P(AXES, None, None),
        P(AXES, None, None),
    )
    out_specs = (P(AXES, None, None), P(AXES, None, None), P(AXES, None))
    body = functools.partial(shards, groups=mesh.shape["group"])
    return jax.shard_map(body, mesh=mesh, in_specs=in_specs, out_specs=out_specs, check_vma=False)
```

time: 92.5 us -> 90.9 us (0.983)
    pallas_call x1, Pallas kernels: 8.85 us -> 7.88 us  [expert(): pl.pallas_call(body, out_shape=jax.ShapeDtypeStruct(arrived.shape, jnp.bf...]
where the time goes in v3:
time: 90.9 us; the launch traced here: 90.8 us
  blocking collectives  59.3 us (65%)
  Pallas kernels  17.7 us (19%)
  waiting for transfers between devices  9.25 us (10%)
  starting transfers between devices  3.83 us (4%)
    all_to_all x2, blocking collectives, exchange(): lax.all_to_all(blocks, EXCHANGE_AXES, split_axis=0, concat_axis=0, tiled=...  59.3 us
    all_to_all x1, waiting for transfers between devices, exchange(): lax.all_to_all(blocks, EXCHANGE_AXES, split_axis=0, concat_axis=0, tiled=...  9.25 us
    pallas_call x1, Pallas kernels, expert(): pl.pallas_call(body, out_shape=jax.ShapeDtypeStruct(arrived.shape, jnp.bf...  7.88 us
    pallas_call x1, Pallas kernels, route(): pl.pallas_call(functools.partial(route_kernel, groups), out_shape=(jax.Sh...  3.95 us
    all_to_all x1, starting transfers between devices, exchange(): lax.all_to_all(blocks, EXCHANGE_AXES, split_axis=0, concat_axis=0, tiled=...  3.83 us
    pallas_call x1, Pallas kernels, finish(): pl.pallas_call(functools.partial(finish_kernel, groups), out_shape=(shape...  2.57 us
    pallas_call x1, Pallas kernels, logit_grad(): pl.pallas_call(functools.partial(logit_grad_kernel, groups), out_shape=(j...  2.29 us
  transfers between devices with their start and end apart: 1, of which 1 were waited for; matrix products, arithmetic and copies ran while one was open for 0% of the time, Pallas kernels for 3%

profile of v3, /device:TPU:1, one launch (start us, length us, event | category | flops | bytes accessed | tf_op | source)
XLA Modules:
  0.0 90.8 jit_solution(9802851286538551428)
XLA Ops:
  0.6 0.0 copy-start
  0.6 4.0 %route.1 = (bf16[32,4,8,640]{3,2,1,0:T(8,128)(2,1)S(1)}, f32[2,256,128]{2,1,0:T(8,128)S(1)}, f32[2,256,128]{2,1,0:T(8,128)S(1)}, bf16[2560,1280]{1,0:T(8,128)(2,1)S(1)}) custom-call(bf16[2,256,1280]{2,1,0:T(8,128)(2,1)} %tokens.1, bf16[2,256,1280]{2,1,0:T(8,128)(2,1)} %upstream.1, bf16[1280,128]{1,0:T(8,128)(2,1)} %key.1, bf16[1,2560,1280]{2,1,0:T(8,128)(2,1)} %weight_hbm.1), custom_call_target="tpu_custom_call" | custom-call | tf_op jit(solution)/shard_map/route/pallas_call | solution.py:138
  4.6 33.5 %all_to_all.15 = bf16[128,8,640]{2,1,0:T(8,128)(2,1)S(1)} all-to-all(bf16[128,8,640]{2,1,0:T(8,128)(2,1)S(1)} %bitcast.9), channel_id=1, replica_groups=mesh['group'=4,'member'=32] {'member','group'}, dimensions={0} | all-to-all | bytes 2621440 | tf_op jit(solution)/shard_map/all_to_all | solution.py:316
  38.1 0.0 copy-done
  38.1 7.9 %expert.1 = bf16[1024,640]{1,0:T(8,128)(2,1)S(1)} custom-call(bf16[1024,640]{1,0:T(8,128)(2,1)S(1)} %bitcast.7, bf16[1,1280,2560]{2,1,0:T(8,128)(2,1)S(1)} %copy-done, bf16[2560,1280]{1,0:T(8,128)(2,1)S(1)} %get-tuple-element.12.refs_2_), custom_call_target="tpu_custom_call" | custom-call | tf_op jit(solution)/shard_map/expert/pallas_call | solution.py:213
  46.0 0.0 copy-start.1
  46.0 0.0 copy-start.2
  46.0 25.8 %all_to_all.16 = bf16[128,8,640]{2,1,0:T(8,128)(2,1)S(1)} all-to-all(bf16[128,8,640]{2,1,0:T(8,128)(2,1)S(1)} %bitcast.8), channel_id=1, replica_groups=mesh['group'=4,'member'=32] {'member','group'}, dimensions={0} | all-to-all | bytes 2621440 | tf_op jit(solution)/shard_map/all_to_all | solution.py:316
  71.8 0.0 copy-done.1
  71.8 0.0 copy-done.2
  71.8 0.0 copy-start.3
  71.8 2.3 %logit_grad.1 = (bf16[2,256,128]{2,1,0:T(8,128)(2,1)S(1)}, bf16[32,4,2,640]{3,2,1,0:T(2,128)(2,1)}) custom-call(bf16[32,4,8,640]{3,2,1,0:T(8,128)(2,1)S(1)} %bitcast.5, bf16[2,256,1280]{2,1,0:T(8,128)(2,1)S(1)} %copy-done.1, bf16[2,256,1280]{2,1,0:T(8,128)(2,1)S(1)} %copy-done.2, f32[2,256,128]{2,1,0:T(8,128)S(1)} %get-tuple-element.13.dispatch, ...), custom_call_target="tpu_custom_call" | custom-call | tf_op jit(solution)/shard_map/logit_grad/pallas_call | solution.py:256
  74.1 3.8 %all-to-all-start.2 = ((bf16[128,2,640]{2,1,0:T(2,128)(2,1)}), bf16[128,2,640]{2,1,0:T(2,128)(2,1)S(1)}, u32[]{:S(2)}, u32[]{:S(2)}) async-start(bf16[128,2,640]{2,1,0:T(2,128)(2,1)} %bitcast.4), calls=%async_computation.2 | async-start | bytes 655360 | tf_op jit(solution)/shard_map/all_to_all | solution.py:316
  78.0 0.0 copy-done.3
  78.0 2.6 %finish.1 = (bf16[2,256,1280]{2,1,0:T(8,128)(2,1)}, bf16[2,256,1280]{2,1,0:T(8,128)(2,1)}) custom-call(bf16[32,4,8,640]{3,2,1,0:T(8,128)(2,1)S(1)} %bitcast.6, f32[2,256,128]{2,1,0:T(8,128)S(1)} %get-tuple-element.13.dispatch, f32[2,256,128]{2,1,0:T(8,128)S(1)} %get-tuple-element.14.combine, bf16[2,256,128]{2,1,0:T(8,128)(2,1)S(1)} %get-tuple-element.15.d_logits, ...), custom_call_target="tpu_custom_call" | custom-call | tf_op jit(solution)/shard_map/finish/pallas_call | solution.py:286
  80.6 9.3 %all-to-all-done.2.terms = bf16[128,2,640]{2,1,0:T(2,128)(2,1)S(1)} async-done(((bf16[128,2,640]{2,1,0:T(2,128)(2,1)}), bf16[128,2,640]{2,1,0:T(2,128)(2,1)S(1)}, u32[]{:S(2)}, u32[]{:S(2)}) %all-to-all-start.2) | async-done | bytes 327712 | tf_op jit(solution)/shard_map/all_to_all | solution.py:316
  89.8 1.0 %key_sum.1 = f32[1,1280]{1,0:T(1,128)} custom-call(bf16[128,2,640]{2,1,0:T(2,128)(2,1)S(1)} %all-to-all-done.2.terms), custom_call_target="tpu_custom_call" | custom-call | tf_op jit(solution)/shard_map/key_sum/pallas_call | solution.py:305
  (1 shorter events, 0.0 us)
Async XLA Ops:
  0.6 37.5 %copy-start = (bf16[1,1280,2560]{2,1,0:T(8,128)(2,1)S(1)}, bf16[1,1280,2560]{2,1,0:T(8,128)(2,1)}, u32[]{:S(2)}) copy-start(bf16[1,1280,2560]{2,1,0:T(8,128)(2,1)} %refs_1_.1) | copy-start | bytes 19660804
  46.0 25.8 %copy-start.1 = (bf16[2,256,1280]{2,1,0:T(8,128)(2,1)S(1)}, bf16[2,256,1280]{2,1,0:T(8,128)(2,1)}, u32[]{:S(2)}) copy-start(bf16[2,256,1280]{2,1,0:T(8,128)(2,1)} %tokens.1) | copy-start | bytes 3932164
  46.0 25.8 %copy-start.2 = (bf16[2,256,1280]{2,1,0:T(8,128)(2,1)S(1)}, bf16[2,256,1280]{2,1,0:T(8,128)(2,1)}, u32[]{:S(2)}) copy-start(bf16[2,256,1280]{2,1,0:T(8,128)(2,1)} %upstream.1) | copy-start | bytes 3932164
  71.8 6.1 %copy-start.3 = (bf16[1280,128]{1,0:T(8,128)(2,1)S(1)}, bf16[1280,128]{1,0:T(8,128)(2,1)}, u32[]{:S(2)}) copy-start(bf16[1280,128]{1,0:T(8,128)(2,1)} %key.1) | copy-start | bytes 983044
  74.1 15.7 %all-to-all-start.2 = ((bf16[128,2,640]{2,1,0:T(2,128)(2,1)}), bf16[128,2,640]{2,1,0:T(2,128)(2,1)S(1)}, u32[]{:S(2)}, u32[]{:S(2)}) async-start(bf16[128,2,640]{2,1,0:T(2,128)(2,1)} %bitcast.4), calls=%async_computation.2 | async-start | bytes 655360 | tf_op jit(solution)/shard_map/all_to_all | solution.py:316

commit v4 on v3

--- a/solution.py
+++ b/solution.py
@@ -38,16 +38,16 @@
     for half in range(HALVES):
         at = (kind * images + image) * HALVES + half
         for block in range(lane_blocks):
-            first = (half * lane_blocks + block) * LANES
+            first = (block * HALVES + half) * LANES
             spread[block, pl.ds(at, peers, stride=per_peer), :] = rows[:, first : first + LANES]
 
 
 def pick(spread, kind, image, images, peers):
     per_peer = KINDS * images * HALVES
     parts = []
-    for half in range(HALVES):
-        at = (kind * images + image) * HALVES + half
-        for block in range(spread.shape[0]):
+    for block in range(spread.shape[0]):
+        for half in range(HALVES):
+            at = (kind * images + image) * HALVES + half
             rows = spread[block, pl.ds(at, peers, stride=per_peer), :]
             parts.append(rows.astype(jnp.bfloat16))
     return jnp.concatenate(parts, axis=1)
@@ -109,8 +109,10 @@
     for image in range(images):
         copies[image].wait()
     slot_weights = []
-    for image in range(images):
-        logits = row_dot(tokens[image], key[...])
+    patches, width = tokens.shape[1:]
+    all_logits = row_dot(tokens[...].reshape(images * patches, width), key[...])
+    for image in range(images):
+        logits = all_logits[image * patches : (image + 1) * patches]
         by_token = jnp.exp(logits - jnp.max(logits, axis=0, keepdims=True))
         by_token = by_token / jnp.sum(by_token, axis=0, keepdims=True)
         dispatch[image] = by_token
@@ -185,9 +187,13 @@
             [pick(spread, kind, image, images, peers) for image in range(images)], axis=0
         )
 
-    def answer(kind, rows):
+    def answer(kind, rows, block=None):
         for image in range(images):
-            place(answers, kind, image, images, rows[image * peers : (image + 1) * peers])
+            own = rows[image * peers : (image + 1) * peers]
+            if block is None:
+                place(answers, kind, image, images, own)
+            else:
+                place(answers.at[pl.ds(block, 1)], kind, image, images, own)
 
     pre = row_dot(rows_of(0), w_in[0])
     square = pre * pre
@@ -200,8 +206,10 @@
     d_act = row_dot_t(rows_of(1), w_out[...])
     d_pre = (d_act * slope).astype(jnp.bfloat16)
     answer(0, row_dot(activated, w_out[...]))
-    answer(1, row_dot_t(d_pre, w_in[0]))
-    for block in range(spread.shape[0]):
+    columns = HALVES * LANES
+    for block in range(spread.shape[0]):
+        rows = slice(block * columns, (block + 1) * columns)
+        answer(1, row_dot_t(d_pre, w_in[0, rows]), block)
         lanes = slice(block * LANES, (block + 1) * LANES)
         sent[:, lanes] = answers[block].astype(jnp.bfloat16)
 
@@ -296,7 +304,9 @@
 
 def key_sum_kernel(terms, total):
     part = terms.shape[2]
-    own = jnp.sum(terms[...].astype(jnp.float32), axis=0)
+    own = jnp.zeros(terms.shape[1:], jnp.float32)
+    for peer in range(terms.shape[0]):
+        own += terms[peer].astype(jnp.float32)
     for half in range(HALVES):
         total[:, half * part : (half + 1) * part] = own[half : half + 1]
 

time: 90.9 us -> 90.5 us (level)
  no operation moved by 1% of the time
where the time goes in v4:
time: 90.5 us; the launch traced here: 90.3 us
  blocking collectives  59.3 us (66%)
  Pallas kernels  17.2 us (19%)
  waiting for transfers between devices  9.25 us (10%)
  starting transfers between devices  3.84 us (4%)
    all_to_all x2, blocking collectives, exchange(): lax.all_to_all(blocks, EXCHANGE_AXES, split_axis=0, concat_axis=0, tiled=...  59.3 us
    all_to_all x1, waiting for transfers between devices, exchange(): lax.all_to_all(blocks, EXCHANGE_AXES, split_axis=0, concat_axis=0, tiled=...  9.25 us
    pallas_call x1, Pallas kernels, expert(): pl.pallas_call(body, out_shape=jax.ShapeDtypeStruct(arrived.shape, jnp.bf...  7.65 us
    pallas_call x1, Pallas kernels, route(): pl.pallas_call(functools.partial(route_kernel, groups), out_shape=(jax.Sh...  3.95 us
    all_to_all x1, starting transfers between devices, exchange(): lax.all_to_all(blocks, EXCHANGE_AXES, split_axis=0, concat_axis=0, tiled=...  3.84 us
    pallas_call x1, Pallas kernels, finish(): pl.pallas_call(functools.partial(finish_kernel, groups), out_shape=(shape...  2.56 us
    pallas_call x1, Pallas kernels, logit_grad(): pl.pallas_call(functools.partial(logit_grad_kernel, groups), out_shape=(j...  2.27 us
  transfers between devices with their start and end apart: 1, of which 1 were waited for; matrix products, arithmetic and copies ran while one was open for 0% of the time, Pallas kernels for 3%

profile of v4, /device:TPU:1, one launch (start us, length us, event | category | flops | bytes accessed | tf_op | source)
XLA Modules:
  0.0 90.3 jit_solution(15786401749619458356)
XLA Ops:
  0.6 0.0 copy-start
  0.6 4.0 %route.1 = (bf16[32,4,8,640]{3,2,1,0:T(8,128)(2,1)S(1)}, f32[2,256,128]{2,1,0:T(8,128)S(1)}, f32[2,256,128]{2,1,0:T(8,128)S(1)}, bf16[2560,1280]{1,0:T(8,128)(2,1)S(1)}) custom-call(bf16[2,256,1280]{2,1,0:T(8,128)(2,1)} %tokens.1, bf16[2,256,1280]{2,1,0:T(8,128)(2,1)} %upstream.1, bf16[1280,128]{1,0:T(8,128)(2,1)} %key.1, bf16[1,2560,1280]{2,1,0:T(8,128)(2,1)} %weight_hbm.1), custom_call_target="tpu_custom_call" | custom-call | tf_op jit(solution)/shard_map/route/pallas_call | solution.py:140
  4.6 33.5 %all_to_all.15 = bf16[128,8,640]{2,1,0:T(8,128)(2,1)S(1)} all-to-all(bf16[128,8,640]{2,1,0:T(8,128)(2,1)S(1)} %bitcast.9), channel_id=1, replica_groups=mesh['group'=4,'member'=32] {'member','group'}, dimensions={0} | all-to-all | bytes 2621440 | tf_op jit(solution)/shard_map/all_to_all | solution.py:326
  38.1 0.0 copy-done
  38.1 7.6 %expert.1 = bf16[1024,640]{1,0:T(8,128)(2,1)S(1)} custom-call(bf16[1024,640]{1,0:T(8,128)(2,1)S(1)} %bitcast.7, bf16[1,1280,2560]{2,1,0:T(8,128)(2,1)S(1)} %copy-done, bf16[2560,1280]{1,0:T(8,128)(2,1)S(1)} %get-tuple-element.12.refs_2_), custom_call_target="tpu_custom_call" | custom-call | tf_op jit(solution)/shard_map/expert/pallas_call | solution.py:221
  45.8 0.0 copy-start.1
  45.8 0.0 copy-start.2
  45.8 25.8 %all_to_all.16 = bf16[128,8,640]{2,1,0:T(8,128)(2,1)S(1)} all-to-all(bf16[128,8,640]{2,1,0:T(8,128)(2,1)S(1)} %bitcast.8), channel_id=1, replica_groups=mesh['group'=4,'member'=32] {'member','group'}, dimensions={0} | all-to-all | bytes 2621440 | tf_op jit(solution)/shard_map/all_to_all | solution.py:326
  71.6 0.0 copy-done.1
  71.6 0.0 copy-done.2
  71.6 0.0 copy-start.3
  71.6 2.3 %logit_grad.1 = (bf16[2,256,128]{2,1,0:T(8,128)(2,1)S(1)}, bf16[32,4,2,640]{3,2,1,0:T(2,128)(2,1)}) custom-call(bf16[32,4,8,640]{3,2,1,0:T(8,128)(2,1)S(1)} %bitcast.5, bf16[2,256,1280]{2,1,0:T(8,128)(2,1)S(1)} %copy-done.1, bf16[2,256,1280]{2,1,0:T(8,128)(2,1)S(1)} %copy-done.2, f32[2,256,128]{2,1,0:T(8,128)S(1)} %get-tuple-element.13.dispatch, ...), custom_call_target="tpu_custom_call" | custom-call | tf_op jit(solution)/shard_map/logit_grad/pallas_call | solution.py:264
  73.9 3.8 %all-to-all-start.2 = ((bf16[128,2,640]{2,1,0:T(2,128)(2,1)}), bf16[128,2,640]{2,1,0:T(2,128)(2,1)S(1)}, u32[]{:S(2)}, u32[]{:S(2)}) async-start(bf16[128,2,640]{2,1,0:T(2,128)(2,1)} %bitcast.4), calls=%async_computation.2 | async-start | bytes 655360 | tf_op jit(solution)/shard_map/all_to_all | solution.py:326
  77.7 0.0 copy-done.3
  77.7 2.6 %finish.1 = (bf16[2,256,1280]{2,1,0:T(8,128)(2,1)}, bf16[2,256,1280]{2,1,0:T(8,128)(2,1)}) custom-call(bf16[32,4,8,640]{3,2,1,0:T(8,128)(2,1)S(1)} %bitcast.6, f32[2,256,128]{2,1,0:T(8,128)S(1)} %get-tuple-element.13.dispatch, f32[2,256,128]{2,1,0:T(8,128)S(1)} %get-tuple-element.14.combine, bf16[2,256,128]{2,1,0:T(8,128)(2,1)S(1)} %get-tuple-element.15.d_logits, ...), custom_call_target="tpu_custom_call" | custom-call | tf_op jit(solution)/shard_map/finish/pallas_call | solution.py:294
  80.3 9.3 %all-to-all-done.2.terms = bf16[128,2,640]{2,1,0:T(2,128)(2,1)S(1)} async-done(((bf16[128,2,640]{2,1,0:T(2,128)(2,1)}), bf16[128,2,640]{2,1,0:T(2,128)(2,1)S(1)}, u32[]{:S(2)}, u32[]{:S(2)}) %all-to-all-start.2) | async-done | bytes 327712 | tf_op jit(solution)/shard_map/all_to_all | solution.py:326
  89.6 0.7 key_sum.1
  (1 shorter events, 0.0 us)
Async XLA Ops:
  0.6 37.5 %copy-start = (bf16[1,1280,2560]{2,1,0:T(8,128)(2,1)S(1)}, bf16[1,1280,2560]{2,1,0:T(8,128)(2,1)}, u32[]{:S(2)}) copy-start(bf16[1,1280,2560]{2,1,0:T(8,128)(2,1)} %refs_1_.1) | copy-start | bytes 19660804
  45.8 25.9 %copy-start.1 = (bf16[2,256,1280]{2,1,0:T(8,128)(2,1)S(1)}, bf16[2,256,1280]{2,1,0:T(8,128)(2,1)}, u32[]{:S(2)}) copy-start(bf16[2,256,1280]{2,1,0:T(8,128)(2,1)} %tokens.1) | copy-start | bytes 3932164
  45.8 25.8 %copy-start.2 = (bf16[2,256,1280]{2,1,0:T(8,128)(2,1)S(1)}, bf16[2,256,1280]{2,1,0:T(8,128)(2,1)}, u32[]{:S(2)}) copy-start(bf16[2,256,1280]{2,1,0:T(8,128)(2,1)} %upstream.1) | copy-start | bytes 3932164
  71.6 6.1 %copy-start.3 = (bf16[1280,128]{1,0:T(8,128)(2,1)S(1)}, bf16[1280,128]{1,0:T(8,128)(2,1)}, u32[]{:S(2)}) copy-start(bf16[1280,128]{1,0:T(8,128)(2,1)} %key.1) | copy-start | bytes 983044
  73.9 15.7 %all-to-all-start.2 = ((bf16[128,2,640]{2,1,0:T(2,128)(2,1)}), bf16[128,2,640]{2,1,0:T(2,128)(2,1)S(1)}, u32[]{:S(2)}, u32[]{:S(2)}) async-start(bf16[128,2,640]{2,1,0:T(2,128)(2,1)} %bitcast.4), calls=%async_computation.2 | async-start | bytes 655360 | tf_op jit(solution)/shard_map/all_to_all | solution.py:326

commit v5 on v4

--- a/solution.py
+++ b/solution.py
@@ -195,16 +195,23 @@
             else:
                 place(answers.at[pl.ds(block, 1)], kind, image, images, own)
 
-    pre = row_dot(rows_of(0), w_in[0])
-    square = pre * pre
-    tanh = jnp.tanh(GELU_SCALE * (pre * (1.0 + GELU_CUBIC * square)))
-    gate = 0.5 * (1.0 + tanh)
-    activated = (pre * gate).astype(jnp.bfloat16)
-    slope = gate + 0.5 * pre * (1.0 - tanh * tanh) * (
-        GELU_SCALE * (1.0 + 3.0 * GELU_CUBIC * square)
-    )
-    d_act = row_dot_t(rows_of(1), w_out[...])
-    d_pre = (d_act * slope).astype(jnp.bfloat16)
+    rows_in, rows_grad = rows_of(0), rows_of(1)
+    activated, d_pre = [], []
+    units = w_out.shape[0] // 2
+    for at in range(2):
+        part = slice(at * units, (at + 1) * units)
+        d_act = row_dot_t(rows_grad, w_out[part])
+        pre = row_dot(rows_in, w_in[0, :, part])
+        square = pre * pre
+        tanh = jnp.tanh(GELU_SCALE * (pre * (1.0 + GELU_CUBIC * square)))
+        gate = 0.5 * (1.0 + tanh)
+        slope = gate + 0.5 * pre * (1.0 - tanh * tanh) * (
+            GELU_SCALE * (1.0 + 3.0 * GELU_CUBIC * square)
+        )
+        activated.append((pre * gate).astype(jnp.bfloat16))
+        d_pre.append((d_act * slope).astype(jnp.bfloat16))
+    activated = jnp.concatenate(activated, axis=1)
+    d_pre = jnp.concatenate(d_pre, axis=1)
     answer(0, row_dot(activated, w_out[...]))
     columns = HALVES * LANES
     for block in range(spread.shape[0]):
@@ -235,7 +242,7 @@
     images, patches, width = tokens.shape
     slots = dispatch.shape[2]
     widen(spread, arrived, groups)
-    total = jnp.zeros((slots, width), jnp.float32)
+    grads = []
     for image in range(images):
         returned = pick(spread, 0, image, images, slots)
         d_slot_in = pick(spread, 1, image, images, slots)
@@ -247,7 +254,10 @@
         both += by_token * (d_dispatch - jnp.sum(by_token * d_dispatch, axis=0, keepdims=True))
         both = both.astype(jnp.bfloat16)
         d_logits[image] = both
-        total += col_dot(both, tokens[image])
+        grads.append(both)
+    total = col_dot(
+        jnp.concatenate(grads, axis=0), tokens[...].reshape(images * patches, width)
+    )
     part = width // HALVES
     members = slots // groups
     for half in range(HALVES):

time: 90.5 us -> 90.3 us (level)
  no operation moved by 1% of the time
where the time goes in v5:
time: 90.3 us; the launch traced here: 90.2 us
  blocking collectives  59.3 us (66%)
  Pallas kernels  17 us (19%)
  waiting for transfers between devices  9.25 us (10%)
  starting transfers between devices  3.83 us (4%)
    all_to_all x2, blocking collectives, exchange(): lax.all_to_all(blocks, EXCHANGE_AXES, split_axis=0, concat_axis=0, tiled=...  59.3 us
    all_to_all x1, waiting for transfers between devices, exchange(): lax.all_to_all(blocks, EXCHANGE_AXES, split_axis=0, concat_axis=0, tiled=...  9.25 us
    pallas_call x1, Pallas kernels, expert(): pl.pallas_call(body, out_shape=jax.ShapeDtypeStruct(arrived.shape, jnp.bf...  7.6 us
    pallas_call x1, Pallas kernels, route(): pl.pallas_call(functools.partial(route_kernel, groups), out_shape=(jax.Sh...  3.95 us
    all_to_all x1, starting transfers between devices, exchange(): lax.all_to_all(blocks, EXCHANGE_AXES, split_axis=0, concat_axis=0, tiled=...  3.83 us
    pallas_call x1, Pallas kernels, finish(): pl.pallas_call(functools.partial(finish_kernel, groups), out_shape=(shape...  2.56 us
    pallas_call x1, Pallas kernels, logit_grad(): pl.pallas_call(functools.partial(logit_grad_kernel, groups), out_shape=(j...  2.2 us
  transfers between devices with their start and end apart: 1, of which 1 were waited for; matrix products, arithmetic and copies ran while one was open for 0% of the time, Pallas kernels for 3%

profile of v5, /device:TPU:1, one launch (start us, length us, event | category | flops | bytes accessed | tf_op | source)
XLA Modules:
  0.0 90.2 jit_solution(17222467366216146346)
XLA Ops:
  0.6 0.0 copy-start
  0.6 4.0 %route.1 = (bf16[32,4,8,640]{3,2,1,0:T(8,128)(2,1)S(1)}, f32[2,256,128]{2,1,0:T(8,128)S(1)}, f32[2,256,128]{2,1,0:T(8,128)S(1)}, bf16[2560,1280]{1,0:T(8,128)(2,1)S(1)}) custom-call(bf16[2,256,1280]{2,1,0:T(8,128)(2,1)} %tokens.1, bf16[2,256,1280]{2,1,0:T(8,128)(2,1)} %upstream.1, bf16[1280,128]{1,0:T(8,128)(2,1)} %key.1, bf16[1,2560,1280]{2,1,0:T(8,128)(2,1)} %weight_hbm.1), custom_call_target="tpu_custom_call" | custom-call | tf_op jit(solution)/shard_map/route/pallas_call | solution.py:140
  4.6 33.5 %all_to_all.15 = bf16[128,8,640]{2,1,0:T(8,128)(2,1)S(1)} all-to-all(bf16[128,8,640]{2,1,0:T(8,128)(2,1)S(1)} %bitcast.9), channel_id=1, replica_groups=mesh['group'=4,'member'=32] {'member','group'}, dimensions={0} | all-to-all | bytes 2621440 | tf_op jit(solution)/shard_map/all_to_all | solution.py:336
  38.1 0.0 copy-done
  38.1 7.6 %expert.1 = bf16[1024,640]{1,0:T(8,128)(2,1)S(1)} custom-call(bf16[1024,640]{1,0:T(8,128)(2,1)S(1)} %bitcast.7, bf16[1,1280,2560]{2,1,0:T(8,128)(2,1)S(1)} %copy-done, bf16[2560,1280]{1,0:T(8,128)(2,1)S(1)} %get-tuple-element.12.refs_2_), custom_call_target="tpu_custom_call" | custom-call | tf_op jit(solution)/shard_map/expert/pallas_call | solution.py:228
  45.7 0.0 copy-start.1
  45.7 0.0 copy-start.2
  45.7 25.8 %all_to_all.16 = bf16[128,8,640]{2,1,0:T(8,128)(2,1)S(1)} all-to-all(bf16[128,8,640]{2,1,0:T(8,128)(2,1)S(1)} %bitcast.8), channel_id=1, replica_groups=mesh['group'=4,'member'=32] {'member','group'}, dimensions={0} | all-to-all | bytes 2621440 | tf_op jit(solution)/shard_map/all_to_all | solution.py:336
  71.6 0.0 copy-done.1
  71.6 0.0 copy-done.2
  71.6 0.0 copy-start.3
  71.6 2.2 %logit_grad.1 = (bf16[2,256,128]{2,1,0:T(8,128)(2,1)S(1)}, bf16[32,4,2,640]{3,2,1,0:T(2,128)(2,1)}) custom-call(bf16[32,4,8,640]{3,2,1,0:T(8,128)(2,1)S(1)} %bitcast.5, bf16[2,256,1280]{2,1,0:T(8,128)(2,1)S(1)} %copy-done.1, bf16[2,256,1280]{2,1,0:T(8,128)(2,1)S(1)} %copy-done.2, f32[2,256,128]{2,1,0:T(8,128)S(1)} %get-tuple-element.13.dispatch, ...), custom_call_target="tpu_custom_call" | custom-call | tf_op jit(solution)/shard_map/logit_grad/pallas_call | solution.py:274
  73.8 3.8 %all-to-all-start.2 = ((bf16[128,2,640]{2,1,0:T(2,128)(2,1)}), bf16[128,2,640]{2,1,0:T(2,128)(2,1)S(1)}, u32[]{:S(2)}, u32[]{:S(2)}) async-start(bf16[128,2,640]{2,1,0:T(2,128)(2,1)} %bitcast.4), calls=%async_computation.2 | async-start | bytes 655360 | tf_op jit(solution)/shard_map/all_to_all | solution.py:336
  77.6 0.0 copy-done.3
  77.6 2.6 %finish.1 = (bf16[2,256,1280]{2,1,0:T(8,128)(2,1)}, bf16[2,256,1280]{2,1,0:T(8,128)(2,1)}) custom-call(bf16[32,4,8,640]{3,2,1,0:T(8,128)(2,1)S(1)} %bitcast.6, f32[2,256,128]{2,1,0:T(8,128)S(1)} %get-tuple-element.13.dispatch, f32[2,256,128]{2,1,0:T(8,128)S(1)} %get-tuple-element.14.combine, bf16[2,256,128]{2,1,0:T(8,128)(2,1)S(1)} %get-tuple-element.15.d_logits, ...), custom_call_target="tpu_custom_call" | custom-call | tf_op jit(solution)/shard_map/finish/pallas_call | solution.py:304
  80.2 9.3 %all-to-all-done.2.terms = bf16[128,2,640]{2,1,0:T(2,128)(2,1)S(1)} async-done(((bf16[128,2,640]{2,1,0:T(2,128)(2,1)}), bf16[128,2,640]{2,1,0:T(2,128)(2,1)S(1)}, u32[]{:S(2)}, u32[]{:S(2)}) %all-to-all-start.2) | async-done | bytes 327712 | tf_op jit(solution)/shard_map/all_to_all | solution.py:336
  89.4 0.7 key_sum.1
  (1 shorter events, 0.0 us)
Async XLA Ops:
  0.6 37.5 %copy-start = (bf16[1,1280,2560]{2,1,0:T(8,128)(2,1)S(1)}, bf16[1,1280,2560]{2,1,0:T(8,128)(2,1)}, u32[]{:S(2)}) copy-start(bf16[1,1280,2560]{2,1,0:T(8,128)(2,1)} %refs_1_.1) | copy-start | bytes 19660804
  45.7 25.8 %copy-start.1 = (bf16[2,256,1280]{2,1,0:T(8,128)(2,1)S(1)}, bf16[2,256,1280]{2,1,0:T(8,128)(2,1)}, u32[]{:S(2)}) copy-start(bf16[2,256,1280]{2,1,0:T(8,128)(2,1)} %tokens.1) | copy-start | bytes 3932164
  45.7 25.8 %copy-start.2 = (bf16[2,256,1280]{2,1,0:T(8,128)(2,1)S(1)}, bf16[2,256,1280]{2,1,0:T(8,128)(2,1)}, u32[]{:S(2)}) copy-start(bf16[2,256,1280]{2,1,0:T(8,128)(2,1)} %upstream.1) | copy-start | bytes 3932164
  71.6 6.0 %copy-start.3 = (bf16[1280,128]{1,0:T(8,128)(2,1)S(1)}, bf16[1280,128]{1,0:T(8,128)(2,1)}, u32[]{:S(2)}) copy-start(bf16[1280,128]{1,0:T(8,128)(2,1)} %key.1) | copy-start | bytes 983044
  73.8 15.7 %all-to-all-start.2 = ((bf16[128,2,640]{2,1,0:T(2,128)(2,1)}), bf16[128,2,640]{2,1,0:T(2,128)(2,1)S(1)}, u32[]{:S(2)}, u32[]{:S(2)}) async-start(bf16[128,2,640]{2,1,0:T(2,128)(2,1)} %bitcast.4), calls=%async_computation.2 | async-start | bytes 655360 | tf_op jit(solution)/shard_map/all_to_all | solution.py:336

commit v6 on v5

--- a/solution.py
+++ b/solution.py
@@ -114,10 +114,10 @@
     for image in range(images):
         logits = all_logits[image * patches : (image + 1) * patches]
         by_token = jnp.exp(logits - jnp.max(logits, axis=0, keepdims=True))
-        by_token = by_token / jnp.sum(by_token, axis=0, keepdims=True)
+        by_token = by_token * (1.0 / jnp.sum(by_token, axis=0, keepdims=True))
         dispatch[image] = by_token
         by_slot = jnp.exp(logits - jnp.max(logits, axis=1, keepdims=True))
-        by_slot = by_slot / jnp.sum(by_slot, axis=1, keepdims=True)
+        by_slot = by_slot * (1.0 / jnp.sum(by_slot, axis=1, keepdims=True))
         combine[image] = by_slot
         slot_weights.append(by_slot.astype(jnp.bfloat16))
         slot_in = col_dot(by_token.astype(jnp.bfloat16), tokens[image])

time: 90.3 us -> 90.3 us (level)
  no operation moved by 1% of the time
where the time goes in v6:
time: 90.3 us; the launch traced here: 90.2 us
  blocking collectives  59.3 us (66%)
  Pallas kernels  17 us (19%)
  waiting for transfers between devices  9.25 us (10%)
  starting transfers between devices  3.83 us (4%)
    all_to_all x2, blocking collectives, exchange(): lax.all_to_all(blocks, EXCHANGE_AXES, split_axis=0, concat_axis=0, tiled=...  59.3 us
    all_to_all x1, waiting for transfers between devices, exchange(): lax.all_to_all(blocks, EXCHANGE_AXES, split_axis=0, concat_axis=0, tiled=...  9.25 us
    pallas_call x1, Pallas kernels, expert(): pl.pallas_call(body, out_shape=jax.ShapeDtypeStruct(arrived.shape, jnp.bf...  7.6 us
    pallas_call x1, Pallas kernels, route(): pl.pallas_call(functools.partial(route_kernel, groups), out_shape=(jax.Sh...  3.95 us
    all_to_all x1, starting transfers between devices, exchange(): lax.all_to_all(blocks, EXCHANGE_AXES, split_axis=0, concat_axis=0, tiled=...  3.83 us
    pallas_call x1, Pallas kernels, finish(): pl.pallas_call(functools.partial(finish_kernel, groups), out_shape=(shape...  2.56 us
    pallas_call x1, Pallas kernels, logit_grad(): pl.pallas_call(functools.partial(logit_grad_kernel, groups), out_shape=(j...  2.2 us
  transfers between devices with their start and end apart: 1, of which 1 were waited for; matrix products, arithmetic and copies ran while one was open for 0% of the time, Pallas kernels for 3%

profile of v6, /device:TPU:1, one launch (start us, length us, event | category | flops | bytes accessed | tf_op | source)
XLA Modules:
  0.0 90.2 jit_solution(17222467366216146346)
XLA Ops:
  0.6 0.0 copy-start
  0.6 4.0 %route.1 = (bf16[32,4,8,640]{3,2,1,0:T(8,128)(2,1)S(1)}, f32[2,256,128]{2,1,0:T(8,128)S(1)}, f32[2,256,128]{2,1,0:T(8,128)S(1)}, bf16[2560,1280]{1,0:T(8,128)(2,1)S(1)}) custom-call(bf16[2,256,1280]{2,1,0:T(8,128)(2,1)} %tokens.1, bf16[2,256,1280]{2,1,0:T(8,128)(2,1)} %upstream.1, bf16[1280,128]{1,0:T(8,128)(2,1)} %key.1, bf16[1,2560,1280]{2,1,0:T(8,128)(2,1)} %weight_hbm.1), custom_call_target="tpu_custom_call" | custom-call | tf_op jit(solution)/shard_map/route/pallas_call | solution.py:140
  4.6 33.5 %all_to_all.15 = bf16[128,8,640]{2,1,0:T(8,128)(2,1)S(1)} all-to-all(bf16[128,8,640]{2,1,0:T(8,128)(2,1)S(1)} %bitcast.9), channel_id=1, replica_groups=mesh['group'=4,'member'=32] {'member','group'}, dimensions={0} | all-to-all | bytes 2621440 | tf_op jit(solution)/shard_map/all_to_all | solution.py:336
  38.1 0.0 copy-done
  38.1 7.6 %expert.1 = bf16[1024,640]{1,0:T(8,128)(2,1)S(1)} custom-call(bf16[1024,640]{1,0:T(8,128)(2,1)S(1)} %bitcast.7, bf16[1,1280,2560]{2,1,0:T(8,128)(2,1)S(1)} %copy-done, bf16[2560,1280]{1,0:T(8,128)(2,1)S(1)} %get-tuple-element.12.refs_2_), custom_call_target="tpu_custom_call" | custom-call | tf_op jit(solution)/shard_map/expert/pallas_call | solution.py:228
  45.7 0.0 copy-start.1
  45.7 0.0 copy-start.2
  45.7 25.8 %all_to_all.16 = bf16[128,8,640]{2,1,0:T(8,128)(2,1)S(1)} all-to-all(bf16[128,8,640]{2,1,0:T(8,128)(2,1)S(1)} %bitcast.8), channel_id=1, replica_groups=mesh['group'=4,'member'=32] {'member','group'}, dimensions={0} | all-to-all | bytes 2621440 | tf_op jit(solution)/shard_map/all_to_all | solution.py:336
  71.6 0.0 copy-done.1
  71.6 0.0 copy-done.2
  71.6 0.0 copy-start.3
  71.6 2.2 %logit_grad.1 = (bf16[2,256,128]{2,1,0:T(8,128)(2,1)S(1)}, bf16[32,4,2,640]{3,2,1,0:T(2,128)(2,1)}) custom-call(bf16[32,4,8,640]{3,2,1,0:T(8,128)(2,1)S(1)} %bitcast.5, bf16[2,256,1280]{2,1,0:T(8,128)(2,1)S(1)} %copy-done.1, bf16[2,256,1280]{2,1,0:T(8,128)(2,1)S(1)} %copy-done.2, f32[2,256,128]{2,1,0:T(8,128)S(1)} %get-tuple-element.13.dispatch, ...), custom_call_target="tpu_custom_call" | custom-call | tf_op jit(solution)/shard_map/logit_grad/pallas_call | solution.py:274
  73.8 3.8 %all-to-all-start.2 = ((bf16[128,2,640]{2,1,0:T(2,128)(2,1)}), bf16[128,2,640]{2,1,0:T(2,128)(2,1)S(1)}, u32[]{:S(2)}, u32[]{:S(2)}) async-start(bf16[128,2,640]{2,1,0:T(2,128)(2,1)} %bitcast.4), calls=%async_computation.2 | async-start | bytes 655360 | tf_op jit(solution)/shard_map/all_to_all | solution.py:336
  77.6 0.0 copy-done.3
  77.6 2.6 %finish.1 = (bf16[2,256,1280]{2,1,0:T(8,128)(2,1)}, bf16[2,256,1280]{2,1,0:T(8,128)(2,1)}) custom-call(bf16[32,4,8,640]{3,2,1,0:T(8,128)(2,1)S(1)} %bitcast.6, f32[2,256,128]{2,1,0:T(8,128)S(1)} %get-tuple-element.13.dispatch, f32[2,256,128]{2,1,0:T(8,128)S(1)} %get-tuple-element.14.combine, bf16[2,256,128]{2,1,0:T(8,128)(2,1)S(1)} %get-tuple-element.15.d_logits, ...), custom_call_target="tpu_custom_call" | custom-call | tf_op jit(solution)/shard_map/finish/pallas_call | solution.py:304
  80.2 9.3 %all-to-all-done.2.terms = bf16[128,2,640]{2,1,0:T(2,128)(2,1)S(1)} async-done(((bf16[128,2,640]{2,1,0:T(2,128)(2,1)}), bf16[128,2,640]{2,1,0:T(2,128)(2,1)S(1)}, u32[]{:S(2)}, u32[]{:S(2)}) %all-to-all-start.2) | async-done | bytes 327712 | tf_op jit(solution)/shard_map/all_to_all | solution.py:336
  89.4 0.7 key_sum.1
  (1 shorter events, 0.0 us)
Async XLA Ops:
  0.6 37.5 %copy-start = (bf16[1,1280,2560]{2,1,0:T(8,128)(2,1)S(1)}, bf16[1,1280,2560]{2,1,0:T(8,128)(2,1)}, u32[]{:S(2)}) copy-start(bf16[1,1280,2560]{2,1,0:T(8,128)(2,1)} %refs_1_.1) | copy-start | bytes 19660804
  45.7 25.8 %copy-start.1 = (bf16[2,256,1280]{2,1,0:T(8,128)(2,1)S(1)}, bf16[2,256,1280]{2,1,0:T(8,128)(2,1)}, u32[]{:S(2)}) copy-start(bf16[2,256,1280]{2,1,0:T(8,128)(2,1)} %tokens.1) | copy-start | bytes 3932164
  45.7 25.8 %copy-start.2 = (bf16[2,256,1280]{2,1,0:T(8,128)(2,1)S(1)}, bf16[2,256,1280]{2,1,0:T(8,128)(2,1)}, u32[]{:S(2)}) copy-start(bf16[2,256,1280]{2,1,0:T(8,128)(2,1)} %upstream.1) | copy-start | bytes 3932164
  71.6 6.0 %copy-start.3 = (bf16[1280,128]{1,0:T(8,128)(2,1)S(1)}, bf16[1280,128]{1,0:T(8,128)(2,1)}, u32[]{:S(2)}) copy-start(bf16[1280,128]{1,0:T(8,128)(2,1)} %key.1) | copy-start | bytes 983044
  73.8 15.7 %all-to-all-start.2 = ((bf16[128,2,640]{2,1,0:T(2,128)(2,1)}), bf16[128,2,640]{2,1,0:T(2,128)(2,1)S(1)}, u32[]{:S(2)}, u32[]{:S(2)}) async-start(bf16[128,2,640]{2,1,0:T(2,128)(2,1)} %bitcast.4), calls=%async_computation.2 | async-start | bytes 655360 | tf_op jit(solution)/shard_map/all_to_all | solution.py:336

commit v7 on v6

--- a/solution.py
+++ b/solution.py
@@ -314,9 +314,13 @@
 
 def key_sum_kernel(terms, total):
     part = terms.shape[2]
-    own = jnp.zeros(terms.shape[1:], jnp.float32)
-    for peer in range(terms.shape[0]):
+    half_way = terms.shape[0] // 2
+    own = terms[0].astype(jnp.float32)
+    rest = terms[half_way].astype(jnp.float32)
+    for peer in range(1, half_way):
         own += terms[peer].astype(jnp.float32)
+        rest += terms[half_way + peer].astype(jnp.float32)
+    own += rest
     for half in range(HALVES):
         total[:, half * part : (half + 1) * part] = own[half : half + 1]
 

time: 90.3 us -> 90.3 us (level)
  no operation moved by 1% of the time
where the time goes in v7:
time: 90.3 us; the launch traced here: 90.1 us
  blocking collectives  59.3 us (66%)
  Pallas kernels  17 us (19%)
  waiting for transfers between devices  9.25 us (10%)
  starting transfers between devices  3.83 us (4%)
    all_to_all x2, blocking collectives, exchange(): lax.all_to_all(blocks, EXCHANGE_AXES, split_axis=0, concat_axis=0, tiled=...  59.3 us
    all_to_all x1, waiting for transfers between devices, exchange(): lax.all_to_all(blocks, EXCHANGE_AXES, split_axis=0, concat_axis=0, tiled=...  9.25 us
    pallas_call x1, Pallas kernels, expert(): pl.pallas_call(body, out_shape=jax.ShapeDtypeStruct(arrived.shape, jnp.bf...  7.6 us
    pallas_call x1, Pallas kernels, route(): pl.pallas_call(functools.partial(route_kernel, groups), out_shape=(jax.Sh...  3.95 us
    all_to_all x1, starting transfers between devices, exchange(): lax.all_to_all(blocks, EXCHANGE_AXES, split_axis=0, concat_axis=0, tiled=...  3.83 us
    pallas_call x1, Pallas kernels, finish(): pl.pallas_call(functools.partial(finish_kernel, groups), out_shape=(shape...  2.56 us
    pallas_call x1, Pallas kernels, logit_grad(): pl.pallas_call(functools.partial(logit_grad_kernel, groups), out_shape=(j...  2.2 us
  transfers between devices with their start and end apart: 1, of which 1 were waited for; matrix products, arithmetic and copies ran while one was open for 0% of the time, Pallas kernels for 3%

profile of v7, /device:TPU:1, one launch (start us, length us, event | category | flops | bytes accessed | tf_op | source)
XLA Modules:
  0.0 90.1 jit_solution(2653187988219759092)
XLA Ops:
  0.6 0.0 copy-start
  0.6 4.0 %route.1 = (bf16[32,4,8,640]{3,2,1,0:T(8,128)(2,1)S(1)}, f32[2,256,128]{2,1,0:T(8,128)S(1)}, f32[2,256,128]{2,1,0:T(8,128)S(1)}, bf16[2560,1280]{1,0:T(8,128)(2,1)S(1)}) custom-call(bf16[2,256,1280]{2,1,0:T(8,128)(2,1)} %tokens.1, bf16[2,256,1280]{2,1,0:T(8,128)(2,1)} %upstream.1, bf16[1280,128]{1,0:T(8,128)(2,1)} %key.1, bf16[1,2560,1280]{2,1,0:T(8,128)(2,1)} %weight_hbm.1), custom_call_target="tpu_custom_call" | custom-call | tf_op jit(solution)/shard_map/route/pallas_call | solution.py:140
  4.6 33.5 %all_to_all.15 = bf16[128,8,640]{2,1,0:T(8,128)(2,1)S(1)} all-to-all(bf16[128,8,640]{2,1,0:T(8,128)(2,1)S(1)} %bitcast.9), channel_id=1, replica_groups=mesh['group'=4,'member'=32] {'member','group'}, dimensions={0} | all-to-all | bytes 2621440 | tf_op jit(solution)/shard_map/all_to_all | solution.py:340
  38.1 0.0 copy-done
  38.1 7.6 %expert.1 = bf16[1024,640]{1,0:T(8,128)(2,1)S(1)} custom-call(bf16[1024,640]{1,0:T(8,128)(2,1)S(1)} %bitcast.7, bf16[1,1280,2560]{2,1,0:T(8,128)(2,1)S(1)} %copy-done, bf16[2560,1280]{1,0:T(8,128)(2,1)S(1)} %get-tuple-element.12.refs_2_), custom_call_target="tpu_custom_call" | custom-call | tf_op jit(solution)/shard_map/expert/pallas_call | solution.py:228
  45.7 0.0 copy-start.1
  45.7 0.0 copy-start.2
  45.7 25.8 %all_to_all.16 = bf16[128,8,640]{2,1,0:T(8,128)(2,1)S(1)} all-to-all(bf16[128,8,640]{2,1,0:T(8,128)(2,1)S(1)} %bitcast.8), channel_id=1, replica_groups=mesh['group'=4,'member'=32] {'member','group'}, dimensions={0} | all-to-all | bytes 2621440 | tf_op jit(solution)/shard_map/all_to_all | solution.py:340
  71.6 0.0 copy-done.1
  71.6 0.0 copy-done.2
  71.6 0.0 copy-start.3
  71.6 2.2 %logit_grad.1 = (bf16[2,256,128]{2,1,0:T(8,128)(2,1)S(1)}, bf16[32,4,2,640]{3,2,1,0:T(2,128)(2,1)}) custom-call(bf16[32,4,8,640]{3,2,1,0:T(8,128)(2,1)S(1)} %bitcast.5, bf16[2,256,1280]{2,1,0:T(8,128)(2,1)S(1)} %copy-done.1, bf16[2,256,1280]{2,1,0:T(8,128)(2,1)S(1)} %copy-done.2, f32[2,256,128]{2,1,0:T(8,128)S(1)} %get-tuple-element.13.dispatch, ...), custom_call_target="tpu_custom_call" | custom-call | tf_op jit(solution)/shard_map/logit_grad/pallas_call | solution.py:274
  73.8 3.8 %all-to-all-start.2 = ((bf16[128,2,640]{2,1,0:T(2,128)(2,1)}), bf16[128,2,640]{2,1,0:T(2,128)(2,1)S(1)}, u32[]{:S(2)}, u32[]{:S(2)}) async-start(bf16[128,2,640]{2,1,0:T(2,128)(2,1)} %bitcast.4), calls=%async_computation.2 | async-start | bytes 655360 | tf_op jit(solution)/shard_map/all_to_all | solution.py:340
  77.6 0.0 copy-done.3
  77.6 2.6 %finish.1 = (bf16[2,256,1280]{2,1,0:T(8,128)(2,1)}, bf16[2,256,1280]{2,1,0:T(8,128)(2,1)}) custom-call(bf16[32,4,8,640]{3,2,1,0:T(8,128)(2,1)S(1)} %bitcast.6, f32[2,256,128]{2,1,0:T(8,128)S(1)} %get-tuple-element.13.dispatch, f32[2,256,128]{2,1,0:T(8,128)S(1)} %get-tuple-element.14.combine, bf16[2,256,128]{2,1,0:T(8,128)(2,1)S(1)} %get-tuple-element.15.d_logits, ...), custom_call_target="tpu_custom_call" | custom-call | tf_op jit(solution)/shard_map/finish/pallas_call | solution.py:304
  80.2 9.3 %all-to-all-done.2.terms = bf16[128,2,640]{2,1,0:T(2,128)(2,1)S(1)} async-done(((bf16[128,2,640]{2,1,0:T(2,128)(2,1)}), bf16[128,2,640]{2,1,0:T(2,128)(2,1)S(1)}, u32[]{:S(2)}, u32[]{:S(2)}) %all-to-all-start.2) | async-done | bytes 327712 | tf_op jit(solution)/shard_map/all_to_all | solution.py:340
  89.4 0.7 key_sum.1
  (1 shorter events, 0.0 us)
Async XLA Ops:
  0.6 37.5 %copy-start = (bf16[1,1280,2560]{2,1,0:T(8,128)(2,1)S(1)}, bf16[1,1280,2560]{2,1,0:T(8,128)(2,1)}, u32[]{:S(2)}) copy-start(bf16[1,1280,2560]{2,1,0:T(8,128)(2,1)} %refs_1_.1) | copy-start | bytes 19660804
  45.7 25.8 %copy-start.1 = (bf16[2,256,1280]{2,1,0:T(8,128)(2,1)S(1)}, bf16[2,256,1280]{2,1,0:T(8,128)(2,1)}, u32[]{:S(2)}) copy-start(bf16[2,256,1280]{2,1,0:T(8,128)(2,1)} %tokens.1) | copy-start | bytes 3932164
  45.7 25.8 %copy-start.2 = (bf16[2,256,1280]{2,1,0:T(8,128)(2,1)S(1)}, bf16[2,256,1280]{2,1,0:T(8,128)(2,1)}, u32[]{:S(2)}) copy-start(bf16[2,256,1280]{2,1,0:T(8,128)(2,1)} %upstream.1) | copy-start | bytes 3932164
  71.6 6.0 %copy-start.3 = (bf16[1280,128]{1,0:T(8,128)(2,1)S(1)}, bf16[1280,128]{1,0:T(8,128)(2,1)}, u32[]{:S(2)}) copy-start(bf16[1280,128]{1,0:T(8,128)(2,1)} %key.1) | copy-start | bytes 983044
  73.8 15.7 %all-to-all-start.2 = ((bf16[128,2,640]{2,1,0:T(2,128)(2,1)}), bf16[128,2,640]{2,1,0:T(2,128)(2,1)S(1)}, u32[]{:S(2)}, u32[]{:S(2)}) async-start(bf16[128,2,640]{2,1,0:T(2,128)(2,1)} %bitcast.4), calls=%async_computation.2 | async-start | bytes 655360 | tf_op jit(solution)/shard_map/all_to_all | solution.py:340
